TPU v7x, 256 devices: a whole 4x4x8 slice. The times are simulated.
256 devices in a mesh: dom: 128 (over y, x, z), feat: 2 (over core).
Axes of the slice: x: 4, y: 4, z: 8, core: 2. Of those that a mesh axis runs over, the one named last changes fastest.
Arguments:
- features: bfloat16 [262144, 512], P('dom', 'feat'), may hold values from -6 to 6
- prev_features: bfloat16 [262144, 512], P('dom', 'feat'), may hold values from -6 to 6
- cotangent: bfloat16 [262144, 512], P('dom', 'feat'), may hold values from -6 to 6
- adjacency: bfloat16 [12288, 128, 128], P('dom'), may hold values from -0.21875 to 0.21875
- tile_cols: int32 [12288], P('dom'), may hold values from 0 to 39, as said below
- send_idx: int32 [16384, 24], P('dom'), may hold values from 0 to 2047, as said below
- send_cnt: int32 [16384], P('dom'), may hold values from 0 to 24, as said below
- recv_cnt: int32 [16384], P('dom'), may hold values from 0 to 24, as said below
- stale_grad: bfloat16 [16384, 24, 512], P('dom', None, 'feat'), may hold values from -4 to 4
- w_self: bfloat16 [512, 512], P('feat'), may hold values from -0.1875 to 0.1875
- w_neigh: bfloat16 [512, 512], P('feat'), may hold values from -0.1875 to 0.1875
- layer_bias: float32 [512], P('feat'), may hold values from -4 to 4
Outputs:
- hidden: bfloat16 [262144, 512], P('dom', 'feat')
- input_grad: bfloat16 [262144, 512], P('dom', 'feat')
- boundary_grad: bfloat16 [16384, 24, 512], P('dom', None, 'feat')
Inputs may be any that keep to these rules, and one draw needn't show every extreme that they name: `tile_cols`: tile t of a partition lies in row block t // 6; column blocks below 16 are the partition's own rows, the others its received slots. `send_idx`: the indices of one row are distinct. `send_cnt`: A partition sends nothing to itself; some partition receives 24 rows from every other partition. recv_cnt[d * 128 + s] = send_cnt[s * 128 + d].
All inputs are finite; a program needn't handle non-finite values.
Results may differ from a plain program's by a relative error of at most 0.019.
The roundings to bfloat16 on the way count: a program that leaves them out, or rounds other values in their place, can miss the bound.
Values may be sent and summed in bfloat16 or wider, within the bound.
A program may use at most 128 MiB of HBM per device.

v0:
```python
import jax
import jax.numpy as jnp
from jax import lax
from jax.sharding import PartitionSpec as P


def per_device(
    features,
    prev_features,
    cotangent,
    adjacency,
    tile_cols,
    send_idx,
    send_cnt,
    recv_cnt,
    stale_grad,
    w_self,
    w_neigh,
    layer_bias,
):
    peer_count = lax.axis_size("dom")
    rows_dev, shard_width = features.shape
    capacity = send_idx.shape[1]
    row_blocks = rows_dev // 128
    per_row = adjacency.shape[0] // row_blocks
    slot_ids = jnp.arange(capacity, dtype=jnp.int32)
    send_valid = slot_ids[None, :] < send_cnt[:, None]
    row_ids = jnp.arange(rows_dev, dtype=jnp.int32)
    sender = (send_idx.reshape(-1)[:, None] == row_ids[None, :]) & send_valid.reshape(-1)[:, None]
    sender = sender.astype(jnp.bfloat16)
    outgoing = jnp.dot(sender, prev_features, preferred_element_type=jnp.float32).astype(
        jnp.bfloat16
    )
    outgoing = outgoing.reshape(peer_count, capacity, shard_width)
    incoming = lax.all_to_all(outgoing, "dom", split_axis=0, concat_axis=0, tiled=True)
    combined = jnp.concatenate(
        [features, incoming.reshape(peer_count * capacity, shard_width)], axis=0
    )
    blocks = combined.reshape(-1, 128, shard_width)
    block_count = blocks.shape[0]
    block_ids = jnp.arange(block_count, dtype=jnp.int32)
    selector = tile_cols[:, None] == block_ids[None, :]
    select_half = selector.astype(jnp.bfloat16)
    picked = jnp.einsum(
        "tc,cjf->tjf", select_half, blocks, preferred_element_type=jnp.float32
    ).astype(jnp.bfloat16)
    picked = picked.reshape(row_blocks, per_row, 128, shard_width)
    square_tiles = adjacency.reshape(row_blocks, per_row, 128, 128)
    aggregate = jnp.einsum(
        "rtij,rtjf->rif", square_tiles, picked, preferred_element_type=jnp.float32
    )
    aggregate = aggregate.reshape(rows_dev, shard_width).astype(jnp.bfloat16)
    partial_sum = jnp.dot(features, w_self, preferred_element_type=jnp.float32)
    partial_sum = partial_sum + jnp.dot(aggregate, w_neigh, preferred_element_type=jnp.float32)
    preact = lax.psum_scatter(partial_sum, "feat", scatter_dimension=1, tiled=True) + layer_bias
    hidden = jnp.maximum(preact, 0.0).astype(jnp.bfloat16)
    pre_grad = jnp.where(preact > 0, cotangent.astype(jnp.float32), 0.0).astype(jnp.bfloat16)
    contract = (((1,), (1,)), ((), ()))
    portion = lax.all_gather(pre_grad, "feat", axis=1, tiled=True)
    self_term = lax.dot_general(portion, w_self, contract, preferred_element_type=jnp.float32)
    neigh_term = lax.dot_general(portion, w_neigh, contract, preferred_element_type=jnp.float32)
    agg_grad = neigh_term.astype(jnp.bfloat16).reshape(row_blocks, 128, shard_width)
    terms = jnp.einsum("rtij,rif->rtjf", square_tiles, agg_grad, preferred_element_type=jnp.float32)
    select_full = selector.astype(jnp.float32)
    comb_grad = jnp.einsum(
        "tc,tjf->cjf",
        select_full,
        terms.reshape(-1, 128, shard_width),
        precision=lax.Precision.HIGHEST,
    )
    returned = lax.all_to_all(stale_grad, "dom", split_axis=0, concat_axis=0, tiled=True)
    back_flat = returned.reshape(-1, shard_width)
    back_sum = lax.dot_general(
        sender, back_flat, (((0,), (0,)), ((), ())), preferred_element_type=jnp.float32
    )
    total_grad = self_term + comb_grad[:row_blocks].reshape(rows_dev, shard_width) + back_sum
    take_valid = (slot_ids[None, :] < recv_cnt[:, None])[..., None]
    fresh_grad = jnp.where(
        take_valid, comb_grad[row_blocks:].reshape(peer_count, capacity, shard_width), 0.0
    )
    return (hidden, total_grad.astype(jnp.bfloat16), fresh_grad.astype(jnp.bfloat16))


def solution(mesh):
    return jax.shard_map(
        per_device,
        mesh=mesh,
        in_specs=(
            P("dom", "feat"),
            P("dom", "feat"),
            P("dom", "feat"),
            P("dom", None, None),
            P("dom"),
            P("dom", None),
            P("dom"),
            P("dom"),
            P("dom", None, "feat"),
            P("feat", None),
            P("feat", None),
            P("feat"),
        ),
        out_specs=(P("dom", "feat"), P("dom", "feat"), P("dom", None, "feat")),
        check_vma=False,
    )
```

profile of v0, /device:TPU:1, one launch (start us, length us, event | category | flops | bytes accessed | tf_op | source)
XLA Modules:
  0.0 188.0 jit_solution(14447690093071736186)
XLA Ops:
  7.2 0.0 copy-start
  7.2 1.0 copy.19
  8.1 0.1 eq.31
  8.2 0.7 iota_compare_fusion.2
  9.0 0.1 lt.40
  9.1 8.0 %fusion.9 = bf16[3072,256]{1,0:T(8,128)(2,1)} fusion(bf16[2048,256]{1,0:T(8,128)(2,1)} %param.13, s32[3072]{0:T(1024)S(1)} %eq.31, pred[3072]{0:T(1024)(128)(4,1)S(1)} %lt.40), kind=kOutput, calls=%fused_computation.8 | convolution fusion | flops 3234594816 | bytes 2636800 | tf_op jit(solution)/shard_map/dot_general | solution.py:31
  17.1 0.0 copy-start.5
  17.1 16.9 %all-to-all-start = ((bf16[128,24,256]{2,1,0:T(8,128)(2,1)}), bf16[128,24,256]{2,1,0:T(8,128)(2,1)}, u32[]{:S(2)}, u32[]{:S(2)}) async-start(bf16[128,24,256]{2,1,0:T(8,128)(2,1)} %bitcast.50), calls=%async_computation | async-start | bytes 3145728 | tf_op jit(solution)/shard_map/all_to_all | solution.py:35
  34.1 0.2 reduce-scatter.2.cloned.1.call-start
  34.3 0.0 copy-done.5
  34.3 3.9 %fusion.21 = f32[2048,512]{1,0:T(8,128)} fusion(bf16[2048,256]{1,0:T(8,128)(2,1)} %param.12, bf16[256,512]{1,0:T(8,128)(2,1)S(1)} %copy-done.5), kind=kOutput, calls=%fused_computation.28 | convolution fusion | flops 536870912 | bytes 5505024 | tf_op jit(solution)/shard_map/dot_general | solution.py:53
  38.2 37.2 %all-to-all-done = bf16[128,24,256]{2,1,0:T(8,128)(2,1)} async-done(((bf16[128,24,256]{2,1,0:T(8,128)(2,1)}), bf16[128,24,256]{2,1,0:T(8,128)(2,1)}, u32[]{:S(2)}, u32[]{:S(2)}) %all-to-all-start) | async-done | bytes 1572896 | tf_op jit(solution)/shard_map/all_to_all | solution.py:35
  75.4 0.0 copy-start.7
  75.4 1.9 %pad_maximum_fusion = bf16[5120,256]{1,0:T(8,128)(2,1)S(1)} fusion(bf16[3072,256]{1,0:T(8,128)(2,1)} %bitcast.2, bf16[2048,256]{1,0:T(8,128)(2,1)} %param.12), kind=kLoop, calls=%fused_computation.14 | loop fusion | flops 5242880 | bytes 5242880 | tf_op jit(solution)/shard_map/concatenate | solution.py:36
  77.3 0.0 copy-done.7
  77.3 2.3 %convolution_convert_fusion = bf16[96,128,256]{2,0,1:T(8,128)(2,1)S(1)} fusion(bf16[40,128,256]{2,1,0:T(8,128)(2,1)S(1)} %bitcast.45, s32[96]{0:T(128)S(1)} %copy-done.7), kind=kOutput, calls=%fused_computation.9 | convolution fusion | flops 254807808 | bytes 8913280 | tf_op jit(solution)/shard_map/tc,cjf->tjf/dot_general | solution.py:44
  79.6 3.7 %copy.21 = bf16[96,128,256]{2,1,0:T(8,128)(2,1)S(1)} copy(bf16[96,128,256]{2,0,1:T(8,128)(2,1)S(1)} %convolution_convert_fusion) | data formatting | bytes 12582912 | tf_op jit(solution)/shard_map/convert_element_type | solution.py:46
  83.2 0.0 copy-done
  83.2 0.0 copy-start.1
  83.3 0.0 copy-start.4
  83.3 1.3 bitcast_convert_fusion
  84.5 0.9 copy-done.1
  85.4 0.0 copy-done.4
  85.5 2.7 %convolution_add_fusion = f32[2048,512]{1,0:T(8,128)} fusion(f32[2048,512]{1,0:T(8,128)S(1)} %copy-done.1, bf16[2048,256]{1,0:T(8,128)(2,1)S(1)} %bitcast.47, bf16[256,512]{1,0:T(8,128)(2,1)S(1)} %copy-done.4), kind=kOutput, calls=%fused_computation.10 | convolution fusion | flops 537919488 | bytes 9699328 | tf_op jit(solution)/shard_map/dot_general | solution.py:54
  88.1 0.0 reduce-scatter.2.cloned.1.call-update
  88.2 0.0 copy-start.8
  88.2 7.3 %all-to-all-start.1 = ((bf16[128,24,256]{2,1,0:T(8,128)(2,1)}), bf16[128,24,256]{2,1,0:T(8,128)(2,1)}, u32[]{:S(2)}, u32[]{:S(2)}) async-start(bf16[128,24,256]{2,1,0:T(8,128)(2,1)} %param.20), calls=%async_computation.2 | async-start | bytes 3145728 | tf_op jit(solution)/shard_map/all_to_all | solution.py:71
  95.5 0.0 copy-start.9
  95.5 0.3 all-gather.2.cloned.1.call-start
  95.7 4.6 %reduce-scatter.2.cloned.1.call-done = f32[2048,256]{1,0:T(8,128)} async-done(((f32[2048,512]{1,0:T(8,128)}), f32[2048,256]{1,0:T(8,128)}) %reduce-scatter.2.cloned.1.call-update) | async-done | bytes 2097168 | tf_op jit(solution)/shard_map/reduce_scatter | solution.py:55
  100.4 0.0 copy-done.8
  100.4 3.6 %select_convert_fusion.1 = (bf16[2048,256]{1,0:T(8,128)(2,1)}, bf16[2048,256]{1,0:T(8,128)(2,1)}) fusion(bf16[2048,256]{1,0:T(8,128)(2,1)} %param.14, f32[2048,256]{1,0:T(8,128)} %reduce-scatter.2.cloned.1.call-done, f32[256]{0:T(256)S(1)} %copy-done.8), kind=kLoop, calls=%fused_computation.19 | loop fusion | flops 3670016 | bytes 5243904 | tf_op jit(solution)/shard_map/convert_element_type | solution.py:57
  104.0 0.0 all-gather.2.cloned.1.call-update
  104.1 0.0 copy-done.9
  104.1 0.1 iota_compare_fusion.1
  104.2 30.9 %all-to-all-done.1 = bf16[128,24,256]{2,1,0:T(8,128)(2,1)} async-done(((bf16[128,24,256]{2,1,0:T(8,128)(2,1)}), bf16[128,24,256]{2,1,0:T(8,128)(2,1)}, u32[]{:S(2)}, u32[]{:S(2)}) %all-to-all-start.1) | async-done | bytes 1572896 | tf_op jit(solution)/shard_map/all_to_all | solution.py:71
  135.1 10.3 %fusion.1 = f32[2048,256]{1,0:T(8,128)} fusion(bf16[3072,256]{1,0:T(8,128)(2,1)} %bitcast.15, s32[3072]{0:T(1024)S(1)} %eq.31, pred[3072]{0:T(1024)(128)(4,1)S(1)} %lt.40), kind=kOutput, calls=%fused_computation.2 | convolution fusion | flops 3233808384 | bytes 3685376 | tf_op jit(solution)/shard_map/dot_general | solution.py:73
  145.4 0.0 all-gather.2.cloned.1.call-done
  145.4 2.3 %convolution_convert_fusion.1 = bf16[2048,256]{1,0:T(8,128)(2,1)S(1)} fusion(bf16[2048,512]{1,0:T(8,128)(2,1)} %all-gather.2.cloned.1.call-done, bf16[256,512]{1,0:T(8,128)(2,1)S(1)} %copy-done.4), kind=kOutput, calls=%fused_computation.17 | convolution fusion | flops 537395200 | bytes 3407872 | tf_op jit(solution)/shard_map/dot_general | solution.py:61
  147.7 6.4 %fusion.22 = f32[16,256,6,128]{3,1,2,0:T(8,128)} fusion(bf16[16,128,256,1]{2,1,3,0:T(8,128)(2,1)S(1)} %bitcast.49, bf16[16,6,128,128]{3,2,1,0:T(8,128)(2,1)S(1)} %bitcast.42), kind=kOutput, calls=%fused_computation.29 | convolution fusion | flops 805306368 | bytes 16777216 | tf_op jit(solution)/shard_map/rtij,rif->rtjf/dot_general | solution.py:63
  154.1 12.7 %copy.23 = f32[96,128,256]{2,0,1:T(8,128)} copy(f32[96,128,256]{1,2,0:T(8,128)} %bitcast.43) | data formatting | bytes 25165824 | tf_op jit(solution)/shard_map/reshape | solution.py:68
  166.8 8.1 %fusion.16 = f32[40,128,256]{2,0,1:T(8,128)S(1)} fusion(f32[96,128,256]{2,0,1:T(8,128)} %copy.23, s32[96]{0:T(128)S(1)} %copy-done.7), kind=kOutput, calls=%fused_computation.25 | convolution fusion | flops 1509953280 | bytes 17826176 | tf_op jit(solution)/shard_map/tc,tjf->cjf/dot_general | solution.py:65
  174.9 0.3 slice.8
  175.2 0.2 slice.9
  175.4 1.2 copy.24
  176.6 0.0 copy-start.2
  176.6 0.0 copy-start.3
  176.7 0.0 copy-start.6
  176.7 0.4 copy.25
  177.0 1.5 select_convert_fusion
  178.5 0.0 copy-done.2
  178.5 0.9 copy-done.3
  179.4 0.0 copy-done.6
  179.4 1.7 fusion.14
Async XLA Ops:
  7.2 76.1 %copy-start = (bf16[96,128,128]{2,1,0:T(8,128)(2,1)S(1)}, bf16[96,128,128]{2,1,0:T(8,128)(2,1)}, u32[]{:S(2)}) copy-start(bf16[96,128,128]{2,1,0:T(8,128)(2,1)} %param.15) | copy-start | bytes 9437188
  17.1 17.2 %copy-start.5 = (bf16[256,512]{1,0:T(8,128)(2,1)S(1)}, bf16[256,512]{1,0:T(8,128)(2,1)}, u32[]{:S(2)}) copy-start(bf16[256,512]{1,0:T(8,128)(2,1)} %param.21) | copy-start | bytes 786436
  17.1 58.3 %all-to-all-start = ((bf16[128,24,256]{2,1,0:T(8,128)(2,1)}), bf16[128,24,256]{2,1,0:T(8,128)(2,1)}, u32[]{:S(2)}, u32[]{:S(2)}) async-start(bf16[128,24,256]{2,1,0:T(8,128)(2,1)} %bitcast.50), calls=%async_computation | async-start | bytes 3145728 | tf_op jit(solution)/shard_map/all_to_all | solution.py:35
  34.1 66.3 %reduce-scatter.2.cloned.1.call-start = ((), (), s32[]{:S(2)}) async-start(), calls=%async_computation.3 | async-start | bytes 6291456 | tf_op jit(solution)/shard_map/reduce_scatter | solution.py:55
  75.4 1.9 %copy-start.7 = (s32[96]{0:T(128)S(1)}, s32[96]{0:T(128)}, u32[]{:S(2)}) copy-start(s32[96]{0:T(128)} %param.16) | copy-start | bytes 1156
  83.2 2.2 %copy-start.1 = (f32[2048,512]{1,0:T(8,128)S(1)}, f32[2048,512]{1,0:T(8,128)}, u32[]{:S(2)}) copy-start(f32[2048,512]{1,0:T(8,128)} %fusion.21) | copy-start | bytes 12582916
  83.3 2.2 %copy-start.4 = (bf16[256,512]{1,0:T(8,128)(2,1)S(1)}, bf16[256,512]{1,0:T(8,128)(2,1)}, u32[]{:S(2)}) copy-start(bf16[256,512]{1,0:T(8,128)(2,1)} %param.22) | copy-start | bytes 786436
  88.2 12.2 %copy-start.8 = (f32[256]{0:T(256)S(1)}, f32[256]{0:T(256)}, u32[]{:S(2)}) copy-start(f32[256]{0:T(256)} %param.23) | copy-start | bytes 3076
  88.2 46.9 %all-to-all-start.1 = ((bf16[128,24,256]{2,1,0:T(8,128)(2,1)}), bf16[128,24,256]{2,1,0:T(8,128)(2,1)}, u32[]{:S(2)}, u32[]{:S(2)}) async-start(bf16[128,24,256]{2,1,0:T(8,128)(2,1)} %param.20), calls=%async_computation.2 | async-start | bytes 3145728 | tf_op jit(solution)/shard_map/all_to_all | solution.py:71
  95.5 8.6 %copy-start.9 = (s32[128]{0:T(128)S(1)}, s32[128]{0:T(128)}, u32[]{:S(2)}) copy-start(s32[128]{0:T(128)} %param.19) | copy-start | bytes 1540
  95.5 49.9 %all-gather.2.cloned.1.call-start = ((), (), s32[]{:S(2)}) async-start(), calls=%async_computation.4 | async-start | bytes 3145728 | tf_op jit(solution)/shard_map/all_gather | solution.py:59
  176.6 1.8 copy-start.2
  176.6 2.8 %copy-start.3 = (f32[2048,256]{1,0:T(8,128)S(1)}, f32[2048,256]{1,0:T(8,128)}, u32[]{:S(2)}) copy-start(f32[2048,256]{1,0:T(8,128)} %fusion.1) | copy-start | bytes 6291460
  176.7 2.8 %copy-start.6 = (bf16[256,512]{1,0:T(8,128)(2,1)S(1)}, bf16[256,512]{1,0:T(8,128)(2,1)}, u32[]{:S(2)}) copy-start(bf16[256,512]{1,0:T(8,128)(2,1)} %param.21) | copy-start | bytes 786436
Sparse Core Ops, SparseCore 0:
  88.3 12.0 reduce-scatter.1
  104.2 17.2 all-gather.1
where the time goes:
time: 190 us; the launch traced here: 188 us
  waiting for transfers between devices  72.8 us (38%)
  matrix products  47 us (25%)
  starting transfers between devices  24.7 us (13%)
  local copies, waits for them, and re-layouts  21.5 us (11%)
  between operations  14.2 us (7%)
  other arithmetic  7.8 us (4%)
    all_to_all x1, waiting for transfers between devices, per_device(): lax.all_to_all(outgoing, 'dom', split_axis=0, concat_axis=0, tiled=True)  37.2 us
    all_to_all x1, waiting for transfers between devices, per_device(): lax.all_to_all(stale_grad, 'dom', split_axis=0, concat_axis=0, tiled=True)  30.9 us
    all_to_all x1, starting transfers between devices, per_device(): lax.all_to_all(outgoing, 'dom', split_axis=0, concat_axis=0, tiled=True)  16.9 us
    reshape x1, local copies, waits for them, and re-layouts, per_device(): terms.reshape(-1, 128, shard_width)  12.7 us
    dot_general x1, matrix products, per_device(): lax.dot_general(sender, back_flat, (((0,), (0,)), ((), ())), preferred_el...  10.3 us
    dot_general x1, matrix products, per_device(): jnp.einsum('tc,tjf->cjf', select_full, terms.reshape(-1, 128, shard_width...  8.11 us
    dot_general x1, matrix products, per_device(): jnp.dot(sender, prev_features, preferred_element_type=jnp.float32)  8.03 us
    all_to_all x1, starting transfers between devices, per_device(): lax.all_to_all(stale_grad, 'dom', split_axis=0, concat_axis=0, tiled=True)  7.27 us
  transfers between devices with their start and end apart: 4, of which 3 were waited for; matrix products, arithmetic and copies ran while one was open for 10% of the time, Pallas kernels for 0%

commit v1 on v0

--- a/solution.py
+++ b/solution.py
@@ -1,7 +1,121 @@
+import functools
+
 import jax
 import jax.numpy as jnp
 from jax import lax
+from jax.experimental import pallas as pl
+from jax.experimental.pallas import tpu as pltpu
 from jax.sharding import PartitionSpec as P
+
+MESH = pl.DeviceIdType.MESH
+PEERS = 128
+CAP = 24
+GROUP = 16
+GROUPS = PEERS // GROUP
+SLOTS = GROUP * CAP
+
+
+def offset_peer(me, i):
+    z, x, y = lax.rem(me, 8), lax.rem(me // 8, 4), me // 32
+    dz, dx, dy = lax.rem(i, 8), lax.rem(i // 8, 4), i // 32
+    return (lax.rem(y + dy, 4) * 4 + lax.rem(x + dx, 4)) * 8 + lax.rem(z + dz, 8)
+
+
+def exchange_kernel(idx_ref, cnt_ref, prev_ref, stale_ref, recv_ref, back_ref, out_buf, send_sem, recv_sem, local_sem):
+    me, feat = lax.axis_index("dom"), lax.axis_index("feat")
+    rows = prev_ref.shape[0]
+    barrier = pltpu.get_barrier_semaphore()
+
+    def greet(i, carry):
+        pl.semaphore_signal(
+            barrier, inc=1, device_id=(offset_peer(me, i), feat), device_id_type=MESH
+        )
+        return carry
+
+    lax.fori_loop(1, PEERS, greet, 0)
+    own = pltpu.make_async_copy(stale_ref.at[me], back_ref.at[me], local_sem)
+    own.start()
+    slot_of = lax.broadcasted_iota(jnp.int32, (CAP, PEERS), 0)
+    idx = jnp.where(slot_of < cnt_ref[...], idx_ref[...], -1).astype(jnp.float32)
+    tiled = jnp.concatenate([idx] * GROUP, axis=0)
+    lane = lax.broadcasted_iota(jnp.int32, (SLOTS, PEERS), 1)
+    place = lax.broadcasted_iota(jnp.int32, (GROUP, CAP, PEERS), 0).reshape(SLOTS, PEERS)
+    node = lax.broadcasted_iota(jnp.int32, (SLOTS, rows), 1)
+
+    def gather(g, carry):
+        i = g * GROUP + place
+        dz, dx, dy = i & 7, (i >> 3) & 3, i >> 5
+        z, x, y = me & 7, (me >> 3) & 3, me >> 5
+        dest = (((y + dy) & 3) * 4 + ((x + dx) & 3)) * 8 + ((z + dz) & 7)
+        column = jnp.sum(jnp.where(lane == dest, tiled, 0.0), axis=1, keepdims=True)
+        pick = (node == column.astype(jnp.int32)).astype(jnp.float32).astype(jnp.bfloat16)
+        sent = jnp.dot(pick, prev_ref[...], preferred_element_type=jnp.float32)
+        out_buf[pl.ds(g * GROUP, GROUP)] = sent.reshape(GROUP, CAP, -1).astype(jnp.bfloat16)
+
+        @pl.when(g == 0)
+        def _():
+            pl.semaphore_wait(barrier, PEERS - 1)
+
+        def send(i, carry):
+            peer = offset_peer(me, i)
+            pltpu.make_async_remote_copy(
+                src_ref=out_buf.at[i],
+                dst_ref=recv_ref.at[me],
+                send_sem=send_sem.at[0],
+                recv_sem=recv_sem.at[0],
+                device_id=(peer, feat),
+                device_id_type=MESH,
+            ).start()
+            return carry
+
+        lax.fori_loop(jnp.maximum(g * GROUP, 1), (g + 1) * GROUP, send, 0)
+        return carry
+
+    lax.fori_loop(0, GROUPS, gather, 0)
+
+    def send_back(i, carry):
+        peer = offset_peer(me, i)
+        pltpu.make_async_remote_copy(
+            src_ref=stale_ref.at[peer],
+            dst_ref=back_ref.at[me],
+            send_sem=send_sem.at[1],
+            recv_sem=recv_sem.at[1],
+            device_id=(peer, feat),
+            device_id_type=MESH,
+        ).start()
+        return carry
+
+    lax.fori_loop(1, PEERS, send_back, 0)
+    own.wait()
+    own = pltpu.make_async_copy(out_buf.at[0], recv_ref.at[me], local_sem)
+    own.start()
+    own.wait()
+    rest = pl.ds(0, PEERS - 1)
+    for a, ref in enumerate((recv_ref, back_ref)):
+        pltpu.make_async_copy(ref.at[rest], ref.at[rest], recv_sem.at[a]).wait()
+        pltpu.make_async_copy(ref.at[rest], ref.at[rest], send_sem.at[a]).wait()
+
+
+def exchange(send_idx, send_cnt, prev_features, stale_grad):
+    width = prev_features.shape[1]
+    shape = jax.ShapeDtypeStruct((PEERS, CAP, width), jnp.bfloat16)
+    vmem = pl.BlockSpec(memory_space=pltpu.VMEM)
+    anywhere = pl.BlockSpec(memory_space=pl.ANY)
+    return pl.pallas_call(
+        exchange_kernel,
+        out_shape=[shape, shape],
+        in_specs=[vmem, vmem, vmem, anywhere],
+        out_specs=[anywhere, anywhere],
+        scratch_shapes=[
+            pltpu.VMEM((PEERS, CAP, width), jnp.bfloat16),
+            pltpu.SemaphoreType.DMA((2,)),
+            pltpu.SemaphoreType.DMA((2,)),
+            pltpu.SemaphoreType.DMA,
+        ],
+        compiler_params=pltpu.CompilerParams(
+            collective_id=0, has_side_effects=True, vmem_limit_bytes=48 << 20
+        ),
+    )(send_idx.T, send_cnt.reshape(1, PEERS), prev_features, stale_grad)
 
 
 def per_device(
@@ -28,11 +142,7 @@
     row_ids = jnp.arange(rows_dev, dtype=jnp.int32)
     sender = (send_idx.reshape(-1)[:, None] == row_ids[None, :]) & send_valid.reshape(-1)[:, None]
     sender = sender.astype(jnp.bfloat16)
-    outgoing = jnp.dot(sender, prev_features, preferred_element_type=jnp.float32).astype(
-        jnp.bfloat16
-    )
-    outgoing = outgoing.reshape(peer_count, capacity, shard_width)
-    incoming = lax.all_to_all(outgoing, "dom", split_axis=0, concat_axis=0, tiled=True)
+    incoming, returned = exchange(send_idx, send_cnt, prev_features, stale_grad)
     combined = jnp.concatenate(
         [features, incoming.reshape(peer_count * capacity, shard_width)], axis=0
     )
@@ -68,7 +178,6 @@
         terms.reshape(-1, 128, shard_width),
         precision=lax.Precision.HIGHEST,
     )
-    returned = lax.all_to_all(stale_grad, "dom", split_axis=0, concat_axis=0, tiled=True)
     back_flat = returned.reshape(-1, shard_width)
     back_sum = lax.dot_general(
         sender, back_flat, (((0,), (0,)), ((), ())), preferred_element_type=jnp.float32

time: 190 us -> 190 us (level)
  Pallas kernels: 0 us -> 84.5 us
  waiting for transfers between devices: 72.8 us -> 24.4 us
  starting transfers between devices: 24.7 us -> 0.26 us
  matrix products: 47 us -> 35.7 us
  local copies, waits for them, and re-layouts: 21.5 us -> 24.9 us
  other arithmetic: 7.8 us -> 5.43 us
    pallas_call x0 -> x1, Pallas kernels: none -> 84.5 us  [exchange(): pl.pallas_call(exchange_kernel, out_shape=[shape, shape], in_specs=[vmem,...]
    all_to_all x2 -> x0, waiting for transfers between devices: 68.1 us -> none  [the longest x1 37.2 us: per_device(): lax.all_to_all(outgoing, 'dom', split_axis=0, concat_axis=0, tiled=True)]
    all_to_all x2 -> x0, starting transfers between devices: 24.2 us -> none  [the longest x1 16.9 us: per_device(): lax.all_to_all(outgoing, 'dom', split_axis=0, concat_axis=0, tiled=True)]
    reduce_scatter x1, waiting for transfers between devices: 4.65 us -> 17.8 us  [per_device(): lax.psum_scatter(partial_sum, 'feat', scatter_dimension=1, tiled=True)]
    dot_general x1 -> x0, matrix products: 8.03 us -> none  [per_device(): jnp.dot(sender, prev_features, preferred_element_type=jnp.float32)]
    all_gather x1, waiting for transfers between devices: 0.01 us -> 6.55 us  [per_device(): portion = lax.all_gather(pre_grad, 'feat', axis=1, tiled=True)]
    unnamed x21 -> x35, local copies, waits for them, and re-layouts: 2.86 us -> 6.18 us
    dot_general x1, matrix products: 3.89 us -> 0.71 us  [per_device(): partial_sum = jnp.dot(features, w_self, preferred_element_type=jnp.float32)]
  transfers between devices with their start and end apart: 4 -> 2, of which waited for: 3 -> 2; matrix products, arithmetic and copies ran while one was open for 10% -> 6% of each run, Pallas kernels for 0% -> 0%
where the time goes in v1:
time: 190 us
  Pallas kernels  84.5 us (44%)
  matrix products  35.7 us (19%)
  local copies, waits for them, and re-layouts  24.9 us (13%)
  waiting for transfers between devices  24.4 us (13%)
  between operations  14.3 us (8%)
  other arithmetic  5.43 us (3%)
    pallas_call x1, Pallas kernels, exchange(): pl.pallas_call(exchange_kernel, out_shape=[shape, shape], in_specs=[vmem,...  84.5 us
    reduce_scatter x1, waiting for transfers between devices, per_device(): lax.psum_scatter(partial_sum, 'feat', scatter_dimension=1, tiled=True)  17.8 us
    reshape x1, local copies, waits for them, and re-layouts, per_device(): terms.reshape(-1, 128, shard_width)  12.8 us
    dot_general x1, matrix products, per_device(): lax.dot_general(sender, back_flat, (((0,), (0,)), ((), ())), preferred_el...  10.3 us
    dot_general x1, matrix products, per_device(): jnp.einsum('tc,tjf->cjf', select_full, terms.reshape(-1, 128, shard_width...  8.11 us
    all_gather x1, waiting for transfers between devices, per_device(): portion = lax.all_gather(pre_grad, 'feat', axis=1, tiled=True)  6.55 us
    dot_general x1, matrix products, per_device(): jnp.einsum('rtij,rif->rtjf', square_tiles, agg_grad, preferred_element_ty...  6.37 us
    unnamed x35, local copies, waits for them, and re-layouts  6.18 us
  transfers between devices with their start and end apart: 2, of which 2 were waited for; matrix products, arithmetic and copies ran while one was open for 6% of the time, Pallas kernels for 0%

profile of v1, /device:TPU:1, one launch (start us, length us, event | category | flops | bytes accessed | tf_op | source)
XLA Modules:
  0.0 189.5 jit_solution(9934805348039913611)
XLA Ops:
  7.2 0.0 copy-start
  7.2 0.0 reduce-scatter.2.cloned.1.call-start
  7.2 0.0 copy-start.1
  7.2 1.5 copy-done.1
  8.8 0.0 copy-start.2
  8.8 1.2 copy-done.2
  10.0 0.0 copy-start.3
  10.0 0.7 copy-done.3
  10.7 0.0 copy-start.5
  10.7 0.7 copy-done.5
  11.4 0.0 copy-start.9
  11.4 84.5 %shard_map.139 = (bf16[128,24,256]{2,1,0:T(8,128)(2,1)S(1)}, bf16[128,24,256]{2,1,0:T(8,128)(2,1)S(1)}) custom-call(s32[24,128]{1,0:T(8,128)S(1)} %bitcast.44, s32[1,128]{1,0:T(1,128)S(1)} %bitcast.45, bf16[2048,256]{1,0:T(8,128)(2,1)S(1)} %copy-done.2, bf16[128,24,256]{2,1,0:T(8,128)(2,1)S(1)} %copy-done.1), custom_call_target="tpu_custom_call" | custom-call | tf_op jit(solution)/shard_map/pallas_call | solution.py:104
  95.9 0.0 copy-start.7
  95.9 0.0 copy-done.9
  95.9 0.0 copy-start.14
  95.9 0.2 pad_maximum_fusion
  96.1 0.9 copy-done.7
  97.0 0.0 copy-done.14
  97.0 2.3 %convolution_convert_fusion = bf16[96,128,256]{2,0,1:T(8,128)(2,1)S(1)} fusion(bf16[40,128,256]{2,1,0:T(8,128)(2,1)S(1)} %bitcast.49, s32[96]{0:T(128)S(1)} %copy-done.14), kind=kOutput, calls=%fused_computation.5 | convolution fusion | flops 254807808 | bytes 8913280 | tf_op jit(solution)/shard_map/tc,cjf->tjf/dot_general | solution.py:154
  99.3 0.0 copy-start.12
  99.3 3.7 %copy.20 = bf16[96,128,256]{2,1,0:T(8,128)(2,1)S(1)} copy(bf16[96,128,256]{2,0,1:T(8,128)(2,1)S(1)} %convolution_convert_fusion) | data formatting | bytes 12582912 | tf_op jit(solution)/shard_map/convert_element_type | solution.py:156
  103.0 0.0 copy-done.12
  103.0 0.7 fusion.14
  103.7 0.0 copy-done
  103.7 0.0 copy-start.11
  103.7 1.3 bitcast_convert_fusion
  105.0 0.0 copy-done.11
  105.0 2.6 %convolution_add_fusion = f32[2048,512]{1,0:T(8,128)} fusion(f32[2048,512]{1,0:T(8,128)S(1)} %fusion.14, bf16[2048,256]{1,0:T(8,128)(2,1)S(1)} %bitcast.51, bf16[256,512]{1,0:T(8,128)(2,1)S(1)} %copy-done.11), kind=kOutput, calls=%fused_computation.6 | convolution fusion | flops 537919488 | bytes 9699328 | tf_op jit(solution)/shard_map/dot_general | solution.py:164
  107.7 0.0 copy-start.15
  107.7 0.0 reduce-scatter.2.cloned.1.call-update
  107.7 0.0 copy-start.4
  107.7 0.0 copy-start.6
  107.7 0.0 copy-start.16
  107.7 0.2 all-gather.2.cloned.1.call-start
  108.0 17.8 %reduce-scatter.2.cloned.1.call-done = f32[2048,256]{1,0:T(8,128)} async-done(((f32[2048,512]{1,0:T(8,128)}), f32[2048,256]{1,0:T(8,128)}) %reduce-scatter.2.cloned.1.call-update) | async-done | bytes 2097168 | tf_op jit(solution)/shard_map/reduce_scatter | solution.py:165
  125.8 0.0 copy-done.15
  125.8 3.6 %select_convert_fusion.1 = (bf16[2048,256]{1,0:T(8,128)(2,1)}, bf16[2048,256]{1,0:T(8,128)(2,1)}) fusion(bf16[2048,256]{1,0:T(8,128)(2,1)} %param.14, f32[2048,256]{1,0:T(8,128)} %reduce-scatter.2.cloned.1.call-done, f32[256]{0:T(256)S(1)} %copy-done.15), kind=kLoop, calls=%fused_computation.15 | loop fusion | flops 3670016 | bytes 5243904 | tf_op jit(solution)/shard_map/convert_element_type | solution.py:167
  129.4 0.0 all-gather.2.cloned.1.call-update
  129.5 0.0 copy-done.4
  129.5 0.1 copy.24
  129.6 0.1 eq.31
  129.7 0.0 copy-done.6
  129.7 0.1 iota_compare_fusion.2
  129.8 0.1 lt.40
  129.9 0.0 copy-done.16
  129.9 0.1 iota_compare_fusion.1
  130.0 10.3 %fusion.1 = f32[2048,256]{1,0:T(8,128)} fusion(bf16[3072,256]{1,0:T(8,128)(2,1)} %bitcast.46, s32[3072]{0:T(1024)S(1)} %eq.31, pred[3072]{0:T(1024)(128)(4,1)S(1)} %lt.40), kind=kOutput, calls=%fused_computation.2 | convolution fusion | flops 3233808384 | bytes 3685376 | tf_op jit(solution)/shard_map/dot_general | solution.py:182
  140.3 6.6 %all-gather.2.cloned.1.call-done = bf16[2048,512]{1,0:T(8,128)(2,1)} async-done(((bf16[2048,256]{1,0:T(8,128)(2,1)}), bf16[2048,512]{1,0:T(8,128)(2,1)}) %all-gather.2.cloned.1.call-update) | async-done | bytes 2097168 | tf_op jit(solution)/shard_map/all_gather | solution.py:169
  146.8 2.3 %convolution_convert_fusion.1 = bf16[2048,256]{1,0:T(8,128)(2,1)S(1)} fusion(bf16[2048,512]{1,0:T(8,128)(2,1)} %all-gather.2.cloned.1.call-done, bf16[256,512]{1,0:T(8,128)(2,1)S(1)} %copy-done.11), kind=kOutput, calls=%fused_computation.13 | convolution fusion | flops 537395200 | bytes 3407872 | tf_op jit(solution)/shard_map/dot_general | solution.py:171
  149.2 6.4 %fusion.15 = f32[16,256,6,128]{3,1,2,0:T(8,128)} fusion(bf16[16,128,256,1]{2,1,3,0:T(8,128)(2,1)S(1)} %bitcast.53, bf16[16,6,128,128]{3,2,1,0:T(8,128)(2,1)S(1)} %bitcast.42), kind=kOutput, calls=%fused_computation.25 | convolution fusion | flops 805306368 | bytes 16777216 | tf_op jit(solution)/shard_map/rtij,rif->rtjf/dot_general | solution.py:173
  155.5 12.8 %copy.22 = f32[96,128,256]{2,0,1:T(8,128)} copy(f32[96,128,256]{1,2,0:T(8,128)} %bitcast.47) | data formatting | bytes 25165824 | tf_op jit(solution)/shard_map/reshape | solution.py:178
  168.4 8.1 %fusion.9 = f32[40,128,256]{2,0,1:T(8,128)S(1)} fusion(f32[96,128,256]{2,0,1:T(8,128)} %copy.22, s32[96]{0:T(128)S(1)} %copy-done.14), kind=kOutput, calls=%fused_computation.21 | convolution fusion | flops 1509953280 | bytes 17826176 | tf_op jit(solution)/shard_map/tc,tjf->cjf/dot_general | solution.py:175
  176.5 0.3 slice.8
  176.8 0.2 slice.9
  177.0 1.2 copy.23
  178.2 0.0 copy-start.8
  178.2 0.0 copy-start.10
  178.2 0.0 copy-start.13
  178.2 0.4 copy.25
  178.6 1.5 select_convert_fusion
  180.0 0.0 copy-done.8
  180.0 0.9 copy-done.10
  181.0 0.0 copy-done.13
  181.0 1.7 fusion.7
Async XLA Ops:
  7.2 96.6 %copy-start = (bf16[96,128,128]{2,1,0:T(8,128)(2,1)S(1)}, bf16[96,128,128]{2,1,0:T(8,128)(2,1)}, u32[]{:S(2)}) copy-start(bf16[96,128,128]{2,1,0:T(8,128)(2,1)} %param.15) | copy-start | bytes 9437188
  7.2 118.6 %reduce-scatter.2.cloned.1.call-start = ((), (), s32[]{:S(2)}) async-start(), calls=%async_computation.1 | async-start | bytes 6291456 | tf_op jit(solution)/shard_map/reduce_scatter | solution.py:165
  7.2 1.6 copy-start.1
  8.8 1.2 copy-start.2
  10.0 0.7 copy-start.3
  10.7 0.7 copy-start.5
  11.4 84.5 %copy-start.9 = (bf16[2048,256]{1,0:T(8,128)(2,1)S(1)}, bf16[2048,256]{1,0:T(8,128)(2,1)}, u32[]{:S(2)}) copy-start(bf16[2048,256]{1,0:T(8,128)(2,1)} %param.12) | copy-start | bytes 3145732
  95.9 1.1 copy-start.7
  95.9 1.1 copy-start.14
  99.3 3.7 %copy-start.12 = (bf16[256,512]{1,0:T(8,128)(2,1)S(1)}, bf16[256,512]{1,0:T(8,128)(2,1)}, u32[]{:S(2)}) copy-start(bf16[256,512]{1,0:T(8,128)(2,1)} %param.21) | copy-start | bytes 786436
  103.7 1.3 copy-start.11
  107.7 18.1 %copy-start.15 = (f32[256]{0:T(256)S(1)}, f32[256]{0:T(256)}, u32[]{:S(2)}) copy-start(f32[256]{0:T(256)} %param.23) | copy-start | bytes 3076
  107.7 21.8 %copy-start.4 = (s32[128,24]{0,1:T(8,128)S(1)}, s32[128,24]{0,1:T(8,128)}, u32[]{:S(2)}) copy-start(s32[128,24]{0,1:T(8,128)} %param.17) | copy-start | bytes 36868
  107.7 21.9 %copy-start.6 = (s32[128]{0:T(128)S(1)}, s32[128]{0:T(128)}, u32[]{:S(2)}) copy-start(s32[128]{0:T(128)} %param.18) | copy-start | bytes 1540
  107.7 22.1 %copy-start.16 = (s32[128]{0:T(128)S(1)}, s32[128]{0:T(128)}, u32[]{:S(2)}) copy-start(s32[128]{0:T(128)} %param.19) | copy-start | bytes 1540
  107.7 39.1 %all-gather.2.cloned.1.call-start = ((), (), s32[]{:S(2)}) async-start(), calls=%async_computation.2 | async-start | bytes 3145728 | tf_op jit(solution)/shard_map/all_gather | solution.py:169
  178.2 1.8 copy-start.8
  178.2 2.8 %copy-start.10 = (f32[2048,256]{1,0:T(8,128)S(1)}, f32[2048,256]{1,0:T(8,128)}, u32[]{:S(2)}) copy-start(f32[2048,256]{1,0:T(8,128)} %fusion.1) | copy-start | bytes 6291460
  178.2 2.8 %copy-start.13 = (bf16[256,512]{1,0:T(8,128)(2,1)S(1)}, bf16[256,512]{1,0:T(8,128)(2,1)}, u32[]{:S(2)}) copy-start(bf16[256,512]{1,0:T(8,128)(2,1)} %param.21) | copy-start | bytes 786436
Sparse Core Ops, SparseCore 0:
  107.8 17.9 reduce-scatter.1
  129.6 17.2 all-gather.1

commit v2 on v1

v2 whole, which is shorter than its diff:
```python
import jax
import jax.numpy as jnp
from jax import lax
from jax.experimental import pallas as pl
from jax.experimental.pallas import tpu as pltpu
from jax.sharding import PartitionSpec as P

MESH = pl.DeviceIdType.MESH
BF16, F32 = jnp.bfloat16, jnp.float32
PEERS = 128
CAP = 24
GROUP = 16
GROUPS = PEERS // GROUP
SLOTS = GROUP * CAP
BLOCK = 128
GROUP_BLOCKS = SLOTS // BLOCK
TPR = 6
CHUNKS = 4
PIECE = 256
CONTRACT_LAST = (((1,), (1,)), ((), ()))
CONTRACT_FIRST = (((0,), (0,)), ((), ()))


def ahead(me, i):
    z, x, y = lax.rem(me, 8), lax.rem(me // 8, 4), me // 32
    dz, dx, dy = lax.rem(i, 8), lax.rem(i // 8, 4), i // 32
    return (lax.rem(y + dy, 4) * 4 + lax.rem(x + dx, 4)) * 8 + lax.rem(z + dz, 8)


def behind(me, i):
    z, x, y = lax.rem(me, 8), lax.rem(me // 8, 4), me // 32
    dz, dx, dy = lax.rem(i, 8), lax.rem(i // 8, 4), i // 32
    return (lax.rem(y + 4 - dy, 4) * 4 + lax.rem(x + 4 - dx, 4)) * 8 + lax.rem(z + 8 - dz, 8)


def layer_kernel(
    tile_ref,
    idx_ref,
    cnt_ref,
    taken_ref,
    bias_ref,
    feat_ref,
    prev_ref,
    cot_ref,
    adj_ref,
    stale_ref,
    ws_ref,
    wn_ref,
    hid_ref,
    grad_ref,
    bnd_ref,
    prev,
    comb,
    feat2,
    cot,
    ws,
    wn,
    bias,
    adj,
    out_buf,
    recv,
    back,
    agg,
    agg2,
    agg_grad,
    total,
    terms,
    sums,
    spread,
    rows_of,
    meta_v,
    meta_s,
    load_sem,
    send_sem,
    recv_sem,
    back_sem,
    pair_send,
    pair_recv,
    out_sem,
):
    me, feat = lax.axis_index("dom"), lax.axis_index("feat")
    nodes = prev.shape[0]
    chunk = nodes // CHUNKS
    blocks = nodes // BLOCK
    barrier = pltpu.get_barrier_semaphore()

    def greet(i, carry):
        pl.semaphore_signal(barrier, inc=1, device_id=(ahead(me, i), feat), device_id_type=MESH)
        return carry

    pl.semaphore_signal(barrier, inc=1, device_id=(me, 1 - feat), device_id_type=MESH)
    lax.fori_loop(1, PEERS, greet, 0)

    loads = [
        pltpu.make_async_copy(src, dst, load_sem.at[n])
        for n, (src, dst) in enumerate(
            (
                (prev_ref, prev),
                (feat_ref, comb.at[pl.ds(0, blocks)]),
                (adj_ref, adj),
                (cot_ref, cot.at[feat]),
                (ws_ref, ws.at[0]),
                (wn_ref, wn.at[0]),
                (stale_ref.at[me], back.at[0]),
            )
        )
    ]
    for load in loads:
        load.start()
    bias[feat] = jnp.broadcast_to(bias_ref[...], bias.shape[1:])

    slot_of = lax.broadcasted_iota(jnp.int32, (CAP, PEERS), 0)
    idx = jnp.where(slot_of < cnt_ref[...], idx_ref[...], -1).astype(F32)
    tiled = jnp.concatenate([idx] * GROUP, axis=0)
    lane = lax.broadcasted_iota(jnp.int32, (SLOTS, PEERS), 1)
    place = lax.broadcasted_iota(jnp.int32, (GROUP, CAP, PEERS), 0).reshape(SLOTS, PEERS)
    node = lax.broadcasted_iota(jnp.int32, (SLOTS, nodes), 1)
    loads[0].wait()

    def gather(g, carry):
        i = g * GROUP + place
        dz, dx, dy = i & 7, (i >> 3) & 3, i >> 5
        z, x, y = me & 7, (me >> 3) & 3, me >> 5
        dest = (((y + dy) & 3) * 4 + ((x + dx) & 3)) * 8 + ((z + dz) & 7)
        column = jnp.sum(jnp.where(lane == dest, tiled, 0.0), axis=1, keepdims=True)
        pick = (node == column.astype(jnp.int32)).astype(F32).astype(BF16)
        sent = jnp.dot(pick, prev[...], preferred_element_type=F32)
        out_buf[pl.ds(g * GROUP, GROUP)] = sent.reshape(GROUP, CAP, -1).astype(BF16)
        rows_of[g] = jnp.transpose(jnp.broadcast_to(column, (SLOTS, PEERS)))[:8]

        @pl.when(g == 0)
        def _():
            pl.semaphore_wait(barrier, PEERS)

        def send(i, carry):
            pltpu.make_async_remote_copy(
                src_ref=out_buf.at[i],
                dst_ref=recv.at[me],
                send_sem=send_sem.at[0],
                recv_sem=recv_sem,
                device_id=(ahead(me, i), feat),
                device_id_type=MESH,
            ).start()
            return carry

        lax.fori_loop(jnp.maximum(g * GROUP, 1), (g + 1) * GROUP, send, 0)
        return carry

    lax.fori_loop(0, GROUPS, gather, 0)
    recv[me] = out_buf[0]

    def to_pair(n, src, dst):
        return pltpu.make_async_remote_copy(
            src_ref=src,
            dst_ref=dst,
            send_sem=pair_send.at[n],
            recv_sem=pair_recv.at[n],
            device_id=(me, 1 - feat),
            device_id_type=MESH,
        )

    pairs = [
        to_pair(CHUNKS, ws_ref, ws.at[1]),
        to_pair(CHUNKS + 1, wn_ref, wn.at[1]),
        to_pair(CHUNKS + 2, bias.at[feat], bias.at[feat]),
        to_pair(CHUNKS + 3, feat_ref, feat2),
        to_pair(CHUNKS + 4, cot_ref, cot.at[feat]),
    ]
    for pair in pairs:
        pair.start()

    def send_back(i, carry):
        peer = behind(me, i)
        pltpu.make_async_remote_copy(
            src_ref=stale_ref.at[peer],
            dst_ref=back.at[i],
            send_sem=send_sem.at[1],
            recv_sem=back_sem.at[i // GROUP],
            device_id=(peer, feat),
            device_id_type=MESH,
        ).start()
        return carry

    lax.fori_loop(1, PEERS, send_back, 0)

    sub = lax.broadcasted_iota(jnp.int32, (BLOCK, BLOCK), 0)
    lanes = lax.broadcasted_iota(jnp.int32, (BLOCK, BLOCK), 1)
    tiles = adj.shape[0]

    def spread_cols(t, carry):
        down, across = carry
        col = tile_ref[t]
        return jnp.where(sub == t, col, down), jnp.where(lanes == t, col, across)

    def count(hits, axis=0):
        return jnp.sum(jnp.where(hits, 1, 0), axis=axis, keepdims=True)

    far = jnp.full((BLOCK, BLOCK), 1000, jnp.int32)
    down, across = lax.fori_loop(0, tiles, spread_cols, (far, far))
    rank = count(across * BLOCK + lanes < down * BLOCK + sub, axis=1)
    at_rank = jnp.where(lanes == rank, 1, 0)
    follows = jnp.where(lanes == rank + 1, 1, 0)
    col_here = jnp.sum(down * at_rank, axis=0, keepdims=True)
    col_before = jnp.sum((down + 1) * follows, axis=0, keepdims=True)
    meta_v[...] = jnp.zeros(meta_v.shape, jnp.int32)
    meta_v[0:1, :] = jnp.sum(sub * at_rank, axis=0, keepdims=True)
    meta_v[1:2, :] = jnp.where(col_here + 1 == col_before, 1, 0)
    meta_v[2:3, :] = jnp.maximum(count(down <= lanes) - 1, 0)
    meta_v[3:4, :] = jnp.minimum(count(down == lanes), 1)
    meta_copy = pltpu.make_async_copy(meta_v, meta_s, out_sem.at[3])
    meta_copy.start()
    meta_copy.wait()

    all_but_one = pl.ds(0, PEERS - 1)
    for load in loads[1:]:
        load.wait()
    pltpu.make_async_copy(recv.at[all_but_one], recv.at[all_but_one], recv_sem).wait()

    def place_rows(g, carry):
        rows = recv[pl.ds(g * GROUP, GROUP)].astype(F32).reshape(SLOTS, -1).astype(BF16)
        comb[pl.ds(blocks + g * GROUP_BLOCKS, GROUP_BLOCKS)] = rows.reshape(GROUP_BLOCKS, BLOCK, -1)
        return carry

    lax.fori_loop(0, GROUPS, place_rows, 0)

    def rows_of_chunk(q):
        return pl.ds(pl.multiple_of(q * chunk, chunk), chunk)

    def agg_pair(q):
        return to_pair(q, agg.at[rows_of_chunk(q)], agg2.at[rows_of_chunk(q)])

    def aggregate(q, carry):
        def row_block(r, carry):
            left = jnp.concatenate([adj[r * TPR + j] for j in range(TPR)], axis=1)
            right = jnp.concatenate(
                [comb[tile_ref[r * TPR + j]] for j in range(TPR)], axis=0
            )
            summed = jnp.dot(left, right, preferred_element_type=F32)
            agg[pl.ds(pl.multiple_of(r * BLOCK, BLOCK), BLOCK)] = summed.astype(BF16)
            return carry

        per_chunk = chunk // BLOCK
        lax.fori_loop(q * per_chunk, (q + 1) * per_chunk, row_block, 0)
        agg_pair(q).start()
        return carry

    lax.fori_loop(0, CHUNKS, aggregate, 0)
    for pair in pairs:
        pair.wait()

    def dense(q, carry):
        agg_pair(q).wait()
        rows = rows_of_chunk(q)
        own = comb[pl.ds(q * (chunk // BLOCK), chunk // BLOCK)].reshape(chunk, -1)
        other = feat2[pl.ds(q * (chunk // BLOCK), chunk // BLOCK)].reshape(chunk, -1)
        neigh_grad = self_grad = None
        for j in range(2):
            cols = slice(j * 256, (j + 1) * 256)
            preact = jnp.dot(own, ws[0, :, cols], preferred_element_type=F32)
            preact += jnp.dot(other, ws[1, :, cols], preferred_element_type=F32)
            preact += jnp.dot(agg[rows, :], wn[0, :, cols], preferred_element_type=F32)
            preact += jnp.dot(agg2[rows, :], wn[1, :, cols], preferred_element_type=F32)
            preact += bias[j][0:1, :]
            pre_grad = jnp.where(preact > 0, cot[j, rows, :].astype(F32), 0.0).astype(BF16)
            cot[j, rows, :] = jnp.maximum(preact, 0.0).astype(BF16)
            part = lax.dot_general(
                pre_grad, wn[0, :, cols], CONTRACT_LAST, preferred_element_type=F32
            )
            neigh_grad = part if j == 0 else neigh_grad + part
            part = lax.dot_general(
                pre_grad, ws[0, :, cols], CONTRACT_LAST, preferred_element_type=F32
            )
            self_grad = part if j == 0 else self_grad + part
        agg_grad[rows, :] = neigh_grad.astype(BF16)
        total[rows, :] = self_grad
        return carry

    lax.fori_loop(0, CHUNKS, dense, 0)
    hid_copy = pltpu.make_async_copy(cot.at[feat], hid_ref, out_sem.at[0])
    hid_copy.start()

    def tile_terms(r, carry):
        left = jnp.concatenate([adj[r * TPR + j] for j in range(TPR)], axis=1)
        right = agg_grad[pl.ds(pl.multiple_of(r * BLOCK, BLOCK), BLOCK), :]
        part = lax.dot_general(left, right, CONTRACT_FIRST, preferred_element_type=F32)
        terms[pl.ds(r * TPR, TPR)] = part.reshape(TPR, BLOCK, -1)
        return carry

    lax.fori_loop(0, blocks, tile_terms, 0)

    def running(i, carry):
        carry = carry * meta_s[1, i].astype(F32) + terms[meta_s[0, i]]
        sums[i] = carry
        return carry

    lax.fori_loop(0, tiles, running, jnp.zeros(terms.shape[1:], F32))

    def column_sum(c):
        return sums[meta_s[2, c]] * meta_s[3, c].astype(F32)

    def add_local(c, carry):
        rows = pl.ds(pl.multiple_of(c * BLOCK, BLOCK), BLOCK)
        total[rows, :] += column_sum(c)
        return carry

    lax.fori_loop(0, blocks, add_local, 0)

    pltpu.make_async_copy(out_buf.at[all_but_one], out_buf.at[all_but_one], send_sem.at[0]).wait()
    slot = lax.broadcasted_iota(jnp.int32, (GROUP, CAP, 256), 1).reshape(SLOTS, 256).astype(F32)
    taken = jnp.broadcast_to(taken_ref[...].astype(F32), (SLOTS, PEERS))

    def boundary(g, carry):
        first = blocks + g * GROUP_BLOCKS
        rows = jnp.concatenate([column_sum(first + n) for n in range(GROUP_BLOCKS)], axis=0)
        limit = jnp.sum(
            jnp.where(lane == g * GROUP + place, taken, 0.0), axis=1, keepdims=True
        )
        rows = jnp.where(slot < limit, rows, 0.0)
        out_buf[pl.ds(g * GROUP, GROUP)] = rows.reshape(GROUP, CAP, -1).astype(BF16)
        return carry

    lax.fori_loop(0, GROUPS, boundary, 0)
    bnd_copy = pltpu.make_async_copy(out_buf, bnd_ref, out_sem.at[1])
    bnd_copy.start()

    def scatter(g, first):
        row = rows_of[g][0:1, :]

        def mark(p, carry):
            at = lax.broadcasted_iota(jnp.int32, (PIECE, SLOTS), 0) + p * PIECE
            hit = jnp.where(at.astype(F32) == row, 1.0, 0.0)
            spread[pl.ds(pl.multiple_of(p * PIECE, PIECE), PIECE), :] = hit.astype(BF16)
            return carry

        lax.fori_loop(0, nodes // PIECE, mark, 0)
        arrived = back.at[pl.ds(0, GROUP - first)]
        pltpu.make_async_copy(arrived, arrived, back_sem.at[g]).wait()
        values = back[pl.ds(g * GROUP, GROUP)].astype(F32).reshape(SLOTS, -1).astype(BF16)

        def add(p, carry):
            rows = pl.ds(pl.multiple_of(p * PIECE, PIECE), PIECE)
            total[rows, :] += jnp.dot(spread[rows, :], values, preferred_element_type=F32)
            return carry

        lax.fori_loop(0, nodes // PIECE, add, 0)

    scatter(0, 1)

    def scatter_group(g, carry):
        scatter(g, 0)
        return carry

    lax.fori_loop(1, GROUPS, scatter_group, 0)
    prev[...] = total[...].astype(BF16)
    grad_copy = pltpu.make_async_copy(prev, grad_ref, out_sem.at[2])
    grad_copy.start()
    pltpu.make_async_copy(back.at[all_but_one], back.at[all_but_one], send_sem.at[1]).wait()
    hid_copy.wait()
    bnd_copy.wait()
    grad_copy.wait()


def per_device(
    features,
    prev_features,
    cotangent,
    adjacency,
    tile_cols,
    send_idx,
    send_cnt,
    recv_cnt,
    stale_grad,
    w_self,
    w_neigh,
    layer_bias,
):
    nodes, width = features.shape
    tiles = adjacency.shape[0]
    rows = jax.ShapeDtypeStruct((nodes, width), BF16)
    slots = jax.ShapeDtypeStruct((PEERS, CAP, width), BF16)
    anywhere = pl.BlockSpec(memory_space=pl.ANY)
    vmem = pl.BlockSpec(memory_space=pltpu.VMEM)
    smem = pl.BlockSpec(memory_space=pltpu.SMEM)
    dma = pltpu.SemaphoreType.DMA
    whole = pltpu.VMEM((nodes, width), BF16)
    return pl.pallas_call(
        layer_kernel,
        out_shape=[rows, rows, slots],
        in_specs=[smem] + [vmem] * 4 + [anywhere] * 7,
        out_specs=[anywhere] * 3,
        scratch_shapes=[
            whole,
            pltpu.VMEM((nodes // BLOCK + GROUPS * GROUP_BLOCKS, BLOCK, width), BF16),
            pltpu.VMEM((nodes // BLOCK, BLOCK, width), BF16),
            pltpu.VMEM((2, nodes, width), BF16),
            pltpu.VMEM((2,) + w_self.shape, BF16),
            pltpu.VMEM((2,) + w_neigh.shape, BF16),
            pltpu.VMEM((2, 8, width), F32),
            pltpu.VMEM(adjacency.shape, BF16),
            pltpu.VMEM((PEERS, CAP, width), BF16),
            pltpu.VMEM((PEERS, CAP, width), BF16),
            pltpu.VMEM((PEERS, CAP, width), BF16),
            whole,
            whole,
            whole,
            pltpu.VMEM((nodes, width), F32),
            pltpu.VMEM((tiles, BLOCK, width), F32),
            pltpu.VMEM((tiles, BLOCK, width), F32),
            pltpu.VMEM((nodes, SLOTS), BF16),
            pltpu.VMEM((GROUPS, 8, SLOTS), F32),
            pltpu.VMEM((8, BLOCK), jnp.int32),
            pltpu.SMEM((8, BLOCK), jnp.int32),
            dma((7,)),
            dma((2,)),
            dma,
            dma((GROUPS,)),
            dma((CHUNKS + 5,)),
            dma((CHUNKS + 5,)),
            dma((4,)),
        ],
        compiler_params=pltpu.CompilerParams(
            collective_id=0, has_side_effects=True, vmem_limit_bytes=62 << 20
        ),
    )(
        tile_cols,
        send_idx.T,
        send_cnt.reshape(1, PEERS),
        recv_cnt.reshape(1, PEERS),
        layer_bias.reshape(1, width),
        features.reshape(nodes // BLOCK, BLOCK, width),
        prev_features,
        cotangent,
        adjacency,
        stale_grad,
        w_self,
        w_neigh,
    )


def solution(mesh):
    return jax.shard_map(
        per_device,
        mesh=mesh,
        in_specs=(
            P("dom", "feat"),
            P("dom", "feat"),
            P("dom", "feat"),
            P("dom", None, None),
            P("dom"),
            P("dom", None),
            P("dom"),
            P("dom"),
            P("dom", None, "feat"),
            P("feat", None),
            P("feat", None),
            P("feat"),
        ),
        out_specs=(P("dom", "feat"), P("dom", "feat"), P("dom", None, "feat")),
        check_vma=False,
    )
```

time: 190 us -> 95.3 us (0.50)
  matrix products: 35.7 us -> 0 us
  waiting for transfers between devices: 24.4 us -> 0 us
  local copies, waits for them, and re-layouts: 24.9 us -> 4.53 us
  between operations: 14.3 us -> 0.66 us
  other arithmetic: 5.43 us -> 0 us
  Pallas kernels: 84.5 us -> 89.9 us
    dot_general x9 -> x0, matrix products: 35.7 us -> none  [the longest x1 10.3 us: per_device(): lax.dot_general(sender, back_flat, (((0,), (0,)), ((), ())), preferred_el...]
    reduce_scatter x1 -> x0, waiting for transfers between devices: 17.8 us -> none  [per_device(): lax.psum_scatter(partial_sum, 'feat', scatter_dimension=1, tiled=True)]
    reshape x1 -> x0, local copies, waits for them, and re-layouts: 12.8 us -> none  [per_device(): terms.reshape(-1, 128, shard_width)]
    all_gather x1 -> x0, waiting for transfers between devices: 6.55 us -> none  [per_device(): portion = lax.all_gather(pre_grad, 'feat', axis=1, tiled=True)]
    pallas_call x1, Pallas kernels: 84.5 us -> 89.9 us  [per_device(): pl.pallas_call(layer_kernel, out_shape=[rows, rows, slots], in_specs=[sme...]
    convert_element_type x2 -> x0, other arithmetic: 5.1 us -> none  [the longest x1 3.64 us: per_device(): jnp.where(preact > 0, cotangent.astype(jnp.float32), 0.0)]
    convert_element_type x1 -> x0, local copies, waits for them, and re-layouts: 3.65 us -> none  [per_device(): picked = jnp.einsum('tc,cjf->tjf', select_half, blocks, preferred_element...]
    slice x4 -> x0, local copies, waits for them, and re-layouts: 2.04 us -> none  [the longest x2 1.53 us: per_device(): comb_grad[:row_blocks].reshape(rows_dev, shard_width)]
  transfers between devices with their start and end apart: 2 -> 0, of which waited for: 2 -> 0; matrix products, arithmetic and copies ran while one was open for 6% -> 0% of each run, Pallas kernels for 0% -> 0%
where the time goes in v2:
time: 95.3 us; the launch traced here: 95.1 us
  Pallas kernels  89.9 us (94%)
  local copies, waits for them, and re-layouts  4.53 us (5%)
    pallas_call x1, Pallas kernels, per_device(): pl.pallas_call(layer_kernel, out_shape=[rows, rows, slots], in_specs=[sme...  89.9 us
    unnamed x7, local copies, waits for them, and re-layouts  4.53 us

profile of v2, /device:TPU:1, one launch (start us, length us, event | category | flops | bytes accessed | tf_op | source)
XLA Modules:
  0.0 95.1 jit_solution(3529647668011879776)
XLA Ops:
  0.6 89.9 %shard_map.139 = (bf16[2048,256]{1,0:T(8,128)(2,1)}, bf16[2048,256]{1,0:T(8,128)(2,1)}, bf16[128,24,256]{2,1,0:T(8,128)(2,1)}) custom-call(s32[96]{0:T(128)} %tile_ref.1, s32[24,128]{1,0:T(8,128)} %bitcast.6, s32[1,128]{1,0:T(1,128)} %bitcast.8, s32[1,128]{1,0:T(1,128)} %bitcast.9, f32[1,256]{1,0:T(1,128)} %bitcast.7, bf16[16,128,256]{2,1,0:T(8,128)(2,1)} %bitcast.5, ...), custom_call_target="tpu_custom_call" | custom-call | tf_op jit(solution)/shard_map/pallas_call | solution.py:386
  90.6 0.0 copy-start.1
  90.6 0.0 copy-start
  90.6 2.4 %copy.18 = bf16[2048,256]{1,0:T(8,128)(2,1)} copy(bf16[2048,256]{1,0:T(8,128)(2,1)} %get-tuple-element.6) | data formatting | bytes 2097152
  93.0 0.0 copy-done.1
  93.0 1.0 %copy.19 = bf16[2048,256]{1,0:T(8,128)(2,1)} copy(bf16[2048,256]{1,0:T(8,128)(2,1)S(1)} %copy-done.1) | data formatting | bytes 2097152
  94.0 0.0 copy-done
  94.0 1.1 %copy.20 = bf16[128,24,256]{2,1,0:T(8,128)(2,1)} copy(bf16[128,24,256]{2,1,0:T(8,128)(2,1)S(1)} %copy-done) | data formatting | bytes 3145728
Async XLA Ops:
  90.6 2.4 %copy-start.1 = (bf16[2048,256]{1,0:T(8,128)(2,1)S(1)}, bf16[2048,256]{1,0:T(8,128)(2,1)}, u32[]{:S(2)}) copy-start(bf16[2048,256]{1,0:T(8,128)(2,1)} %get-tuple-element.7) | copy-start | bytes 3145732
  90.6 3.4 %copy-start = (bf16[128,24,256]{2,1,0:T(8,128)(2,1)S(1)}, bf16[128,24,256]{2,1,0:T(8,128)(2,1)}, u32[]{:S(2)}) copy-start(bf16[128,24,256]{2,1,0:T(8,128)(2,1)} %get-tuple-element.8) | copy-start | bytes 4718596

commit v3 on v2

--- a/solution.py
+++ b/solution.py
@@ -16,29 +16,30 @@
 GROUP_BLOCKS = SLOTS // BLOCK
 TPR = 6
 CHUNKS = 4
+PARTS = 2
 PIECE = 256
 CONTRACT_LAST = (((1,), (1,)), ((), ()))
 CONTRACT_FIRST = (((0,), (0,)), ((), ()))
 
 
-def ahead(me, i):
+def torus(me, sign):
     z, x, y = lax.rem(me, 8), lax.rem(me // 8, 4), me // 32
-    dz, dx, dy = lax.rem(i, 8), lax.rem(i // 8, 4), i // 32
-    return (lax.rem(y + dy, 4) * 4 + lax.rem(x + dx, 4)) * 8 + lax.rem(z + dz, 8)
-
-
-def behind(me, i):
-    z, x, y = lax.rem(me, 8), lax.rem(me // 8, 4), me // 32
-    dz, dx, dy = lax.rem(i, 8), lax.rem(i // 8, 4), i // 32
-    return (lax.rem(y + 4 - dy, 4) * 4 + lax.rem(x + 4 - dx, 4)) * 8 + lax.rem(z + 8 - dz, 8)
+
+    def column(c):
+        dy, dx = c // 4, lax.rem(c, 4)
+        if sign < 0:
+            dy, dx = 4 - dy, 4 - dx
+        return (lax.rem(y + dy, 4) * 4 + lax.rem(x + dx, 4)) * 8
+
+    return column, [lax.rem(z + 8 + sign * dz, 8) for dz in range(8)]
 
 
 def layer_kernel(
-    tile_ref,
-    idx_ref,
-    cnt_ref,
-    taken_ref,
-    bias_ref,
+    tile_hbm,
+    idx_hbm,
+    cnt_hbm,
+    taken_hbm,
+    bias_hbm,
     feat_ref,
     prev_ref,
     cot_ref,
@@ -49,6 +50,11 @@
     hid_ref,
     grad_ref,
     bnd_ref,
+    tile_ref,
+    idx_ref,
+    cnt_ref,
+    taken_ref,
+    bias_ref,
     prev,
     comb,
     feat2,
@@ -84,18 +90,27 @@
     blocks = nodes // BLOCK
     barrier = pltpu.get_barrier_semaphore()
 
-    def greet(i, carry):
-        pl.semaphore_signal(barrier, inc=1, device_id=(ahead(me, i), feat), device_id_type=MESH)
-        return carry
-
-    pl.semaphore_signal(barrier, inc=1, device_id=(me, 1 - feat), device_id_type=MESH)
-    lax.fori_loop(1, PEERS, greet, 0)
+    column_ahead, z_ahead = torus(me, 1)
+    column_behind, z_behind = torus(me, -1)
+
+    def greet(c, carry):
+        base = column_ahead(c)
+        for dz in range(8):
+            pl.semaphore_signal(
+                barrier, inc=1, device_id=(base + z_ahead[dz], feat), device_id_type=MESH
+            )
+        return carry
 
     loads = [
         pltpu.make_async_copy(src, dst, load_sem.at[n])
         for n, (src, dst) in enumerate(
             (
                 (prev_ref, prev),
+                (idx_hbm, idx_ref),
+                (cnt_hbm, cnt_ref),
+                (tile_hbm, tile_ref),
+                (taken_hbm, taken_ref),
+                (bias_hbm, bias_ref),
                 (feat_ref, comb.at[pl.ds(0, blocks)]),
                 (adj_ref, adj),
                 (cot_ref, cot.at[feat]),
@@ -105,9 +120,21 @@
             )
         )
     ]
-    for load in loads:
+    for load in loads[:3]:
         load.start()
-    bias[feat] = jnp.broadcast_to(bias_ref[...], bias.shape[1:])
+    pl.semaphore_signal(barrier, inc=1, device_id=(me, 1 - feat), device_id_type=MESH)
+    for dz in range(1, 8):
+        pl.semaphore_signal(
+            barrier,
+            inc=1,
+            device_id=(column_ahead(0) + z_ahead[dz], feat),
+            device_id_type=MESH,
+        )
+    lax.fori_loop(1, PEERS // 8, greet, 0)
+    for load in loads[3:]:
+        load.start()
+    for load in loads[1:3]:
+        load.wait()
 
     slot_of = lax.broadcasted_iota(jnp.int32, (CAP, PEERS), 0)
     idx = jnp.where(slot_of < cnt_ref[...], idx_ref[...], -1).astype(F32)
@@ -132,18 +159,22 @@
         def _():
             pl.semaphore_wait(barrier, PEERS)
 
-        def send(i, carry):
+        def send(base, i, dz):
             pltpu.make_async_remote_copy(
                 src_ref=out_buf.at[i],
                 dst_ref=recv.at[me],
                 send_sem=send_sem.at[0],
                 recv_sem=recv_sem,
-                device_id=(ahead(me, i), feat),
+                device_id=(base + z_ahead[dz], feat),
                 device_id_type=MESH,
             ).start()
-            return carry
-
-        lax.fori_loop(jnp.maximum(g * GROUP, 1), (g + 1) * GROUP, send, 0)
+
+        for half in range(2):
+            base = column_ahead(2 * g + half)
+            if half == 0:
+                pl.when(g > 0)(lambda: send(base, g * GROUP, 0))
+            for dz in range(1 - half, 8):
+                send(base, g * GROUP + half * 8 + dz, dz)
         return carry
 
     lax.fori_loop(0, GROUPS, gather, 0)
@@ -159,6 +190,9 @@
             device_id_type=MESH,
         )
 
+    for load in loads[3:6]:
+        load.wait()
+    bias[feat] = jnp.broadcast_to(bias_ref[...], bias.shape[1:])
     pairs = [
         to_pair(CHUNKS, ws_ref, ws.at[1]),
         to_pair(CHUNKS + 1, wn_ref, wn.at[1]),
@@ -169,19 +203,25 @@
     for pair in pairs:
         pair.start()
 
-    def send_back(i, carry):
-        peer = behind(me, i)
-        pltpu.make_async_remote_copy(
-            src_ref=stale_ref.at[peer],
-            dst_ref=back.at[i],
-            send_sem=send_sem.at[1],
-            recv_sem=back_sem.at[i // GROUP],
-            device_id=(peer, feat),
-            device_id_type=MESH,
-        ).start()
-        return carry
-
-    lax.fori_loop(1, PEERS, send_back, 0)
+    def send_back(c, first):
+        base = column_behind(c)
+        for dz in range(first, 8):
+            peer = base + z_behind[dz]
+            pltpu.make_async_remote_copy(
+                src_ref=stale_ref.at[peer],
+                dst_ref=back.at[c * 8 + dz],
+                send_sem=send_sem.at[1],
+                recv_sem=back_sem.at[c // 2],
+                device_id=(peer, feat),
+                device_id_type=MESH,
+            ).start()
+
+    def send_back_column(c, carry):
+        send_back(c, 0)
+        return carry
+
+    send_back(0, 1)
+    lax.fori_loop(1, PEERS // 8, send_back_column, 0)
 
     sub = lax.broadcasted_iota(jnp.int32, (BLOCK, BLOCK), 0)
     lanes = lax.broadcasted_iota(jnp.int32, (BLOCK, BLOCK), 1)
@@ -212,7 +252,7 @@
     meta_copy.wait()
 
     all_but_one = pl.ds(0, PEERS - 1)
-    for load in loads[1:]:
+    for load in loads[6:]:
         load.wait()
     pltpu.make_async_copy(recv.at[all_but_one], recv.at[all_but_one], recv_sem).wait()
 
@@ -323,7 +363,11 @@
     bnd_copy = pltpu.make_async_copy(out_buf, bnd_ref, out_sem.at[1])
     bnd_copy.start()
 
-    def scatter(g, first):
+    def out_piece(p):
+        rows = pl.ds(pl.multiple_of(p * PIECE, PIECE), PIECE)
+        return pltpu.make_async_copy(prev.at[rows], grad_ref.at[rows], out_sem.at[2])
+
+    def scatter(g, first, last):
         row = rows_of[g][0:1, :]
 
         def mark(p, carry):
@@ -339,25 +383,52 @@
 
         def add(p, carry):
             rows = pl.ds(pl.multiple_of(p * PIECE, PIECE), PIECE)
-            total[rows, :] += jnp.dot(spread[rows, :], values, preferred_element_type=F32)
+            added = total[rows, :] + jnp.dot(spread[rows, :], values, preferred_element_type=F32)
+            if last:
+                prev[rows, :] = added.astype(BF16)
+                out_piece(p).start()
+            else:
+                total[rows, :] = added
             return carry
 
         lax.fori_loop(0, nodes // PIECE, add, 0)
 
-    scatter(0, 1)
+    scatter(0, 1, False)
 
     def scatter_group(g, carry):
-        scatter(g, 0)
-        return carry
-
-    lax.fori_loop(1, GROUPS, scatter_group, 0)
-    prev[...] = total[...].astype(BF16)
-    grad_copy = pltpu.make_async_copy(prev, grad_ref, out_sem.at[2])
-    grad_copy.start()
+        scatter(g, 0, False)
+        return carry
+
+    lax.fori_loop(1, GROUPS - 1, scatter_group, 0)
+    scatter(GROUPS - 1, 0, True)
     pltpu.make_async_copy(back.at[all_but_one], back.at[all_but_one], send_sem.at[1]).wait()
     hid_copy.wait()
     bnd_copy.wait()
-    grad_copy.wait()
+    pltpu.make_async_copy(prev, grad_ref, out_sem.at[2]).wait()
+
+
+def hand_over(
+    hid_in, grad_in, bnd_in, hid_out, grad_out, bnd_out, hid, grad, bnd, load_sem, store_sem
+):
+    loads, stores = [], []
+    triples = ((hid_in, hid, hid_out), (grad_in, grad, grad_out), (bnd_in, bnd, bnd_out))
+    for n, (src, held, dst) in enumerate(triples):
+        step = held.shape[0] // PARTS
+        for part in range(PARTS):
+            piece = pl.ds(part * step, step)
+            loads.append(
+                pltpu.make_async_copy(src.at[piece], held.at[piece], load_sem.at[n, part])
+            )
+            stores.append(
+                pltpu.make_async_copy(held.at[piece], dst.at[piece], store_sem.at[n, part])
+            )
+    for load in loads:
+        load.start()
+    for load, store in zip(loads, stores):
+        load.wait()
+        store.start()
+    for store in stores:
+        store.wait()
 
 
 def per_device(
@@ -379,16 +450,19 @@
     rows = jax.ShapeDtypeStruct((nodes, width), BF16)
     slots = jax.ShapeDtypeStruct((PEERS, CAP, width), BF16)
     anywhere = pl.BlockSpec(memory_space=pl.ANY)
-    vmem = pl.BlockSpec(memory_space=pltpu.VMEM)
-    smem = pl.BlockSpec(memory_space=pltpu.SMEM)
     dma = pltpu.SemaphoreType.DMA
     whole = pltpu.VMEM((nodes, width), BF16)
-    return pl.pallas_call(
+    results = pl.pallas_call(
         layer_kernel,
         out_shape=[rows, rows, slots],
-        in_specs=[smem] + [vmem] * 4 + [anywhere] * 7,
+        in_specs=[anywhere] * 12,
         out_specs=[anywhere] * 3,
         scratch_shapes=[
+            pltpu.SMEM(tile_cols.shape, jnp.int32),
+            pltpu.VMEM((CAP, PEERS), jnp.int32),
+            pltpu.VMEM((1, PEERS), jnp.int32),
+            pltpu.VMEM((1, PEERS), jnp.int32),
+            pltpu.VMEM((1, width), F32),
             whole,
             pltpu.VMEM((nodes // BLOCK + GROUPS * GROUP_BLOCKS, BLOCK, width), BF16),
             pltpu.VMEM((nodes // BLOCK, BLOCK, width), BF16),
@@ -410,7 +484,7 @@
             pltpu.VMEM((GROUPS, 8, SLOTS), F32),
             pltpu.VMEM((8, BLOCK), jnp.int32),
             pltpu.SMEM((8, BLOCK), jnp.int32),
-            dma((7,)),
+            dma((12,)),
             dma((2,)),
             dma,
             dma((GROUPS,)),
@@ -435,6 +509,20 @@
         w_self,
         w_neigh,
     )
+    return pl.pallas_call(
+        hand_over,
+        out_shape=[rows, rows, slots],
+        in_specs=[anywhere] * 3,
+        out_specs=[anywhere] * 3,
+        scratch_shapes=[
+            whole,
+            whole,
+            pltpu.VMEM((PEERS, CAP, width), BF16),
+            dma((3, PARTS)),
+            dma((3, PARTS)),
+        ],
+        compiler_params=pltpu.CompilerParams(vmem_limit_bytes=62 << 20),
+    )(*results)
 
 
 def solution(mesh):

time: 95.3 us -> 90.1 us (0.945)
  local copies, waits for them, and re-layouts: 4.53 us -> 0 us
    unnamed x7 -> x0, local copies, waits for them, and re-layouts: 4.53 us -> none
    pallas_call x1 -> x2, Pallas kernels: 89.9 us -> 89.3 us  [the longest x1 86.2 us: per_device(): pl.pallas_call(layer_kernel, out_shape=[rows, rows, slots], in_specs=[any...]
where the time goes in v3:
time: 90.1 us; the launch traced here: 90 us
  Pallas kernels  89.3 us (99%)
    pallas_call x1, Pallas kernels, per_device(): pl.pallas_call(layer_kernel, out_shape=[rows, rows, slots], in_specs=[any...  86.2 us
    pallas_call x1, Pallas kernels, per_device(): pl.pallas_call(hand_over, out_shape=[rows, rows, slots], in_specs=[anywhe...  3.11 us

profile of v3, /device:TPU:1, one launch (start us, length us, event | category | flops | bytes accessed | tf_op | source)
XLA Modules:
  0.0 90.0 jit_solution(5869201717415317108)
XLA Ops:
  0.6 86.2 %shard_map.139 = (bf16[2048,256]{1,0:T(8,128)(2,1)}, bf16[2048,256]{1,0:T(8,128)(2,1)}, bf16[128,24,256]{2,1,0:T(8,128)(2,1)}) custom-call(s32[96]{0:T(128)} %tile_hbm.1, s32[24,128]{1,0:T(8,128)} %bitcast.6, s32[1,128]{1,0:T(1,128)} %bitcast.8, s32[1,128]{1,0:T(1,128)} %bitcast.9, f32[1,256]{1,0:T(1,128)} %bitcast.7, bf16[16,128,256]{2,1,0:T(8,128)(2,1)} %bitcast.5, ...), custom_call_target="tpu_custom_call" | custom-call | tf_op jit(solution)/shard_map/pallas_call | solution.py:455
  86.9 3.1 %shard_map.140 = (bf16[2048,256]{1,0:T(8,128)(2,1)}, bf16[2048,256]{1,0:T(8,128)(2,1)}, bf16[128,24,256]{2,1,0:T(8,128)(2,1)}) custom-call(bf16[2048,256]{1,0:T(8,128)(2,1)} %get-tuple-element.6.hid_in, bf16[2048,256]{1,0:T(8,128)(2,1)} %get-tuple-element.7.grad_in, bf16[128,24,256]{2,1,0:T(8,128)(2,1)} %get-tuple-element.8.bnd_in), custom_call_target="tpu_custom_call" | custom-call | tf_op jit(solution)/shard_map/pallas_call | solution.py:512

commit v4 on v3

--- a/solution.py
+++ b/solution.py
@@ -16,8 +16,12 @@
 GROUP_BLOCKS = SLOTS // BLOCK
 TPR = 6
 CHUNKS = 4
-PARTS = 2
+FINISH_MB = 6
 PIECE = 256
+HOPS = [[min(c // 4, 4 - c // 4) + min(c % 4, 4 - c % 4) + min(z, 8 - z) for z in range(8)] for c in range(16)]
+FAR_FIRST = sorted(
+    ((c, dz) for c in range(16) for dz in range(8) if c or dz), key=lambda at: -HOPS[at[0]][at[1]]
+)
 CONTRACT_LAST = (((1,), (1,)), ((), ()))
 CONTRACT_FIRST = (((0,), (0,)), ((), ()))
 
@@ -48,8 +52,10 @@
     ws_ref,
     wn_ref,
     hid_ref,
-    grad_ref,
     bnd_ref,
+    total_ref,
+    spread_ref,
+    last_ref,
     tile_ref,
     idx_ref,
     cnt_ref,
@@ -93,14 +99,6 @@
     column_ahead, z_ahead = torus(me, 1)
     column_behind, z_behind = torus(me, -1)
 
-    def greet(c, carry):
-        base = column_ahead(c)
-        for dz in range(8):
-            pl.semaphore_signal(
-                barrier, inc=1, device_id=(base + z_ahead[dz], feat), device_id_type=MESH
-            )
-        return carry
-
     loads = [
         pltpu.make_async_copy(src, dst, load_sem.at[n])
         for n, (src, dst) in enumerate(
@@ -123,14 +121,10 @@
     for load in loads[:3]:
         load.start()
     pl.semaphore_signal(barrier, inc=1, device_id=(me, 1 - feat), device_id_type=MESH)
-    for dz in range(1, 8):
-        pl.semaphore_signal(
-            barrier,
-            inc=1,
-            device_id=(column_ahead(0) + z_ahead[dz], feat),
-            device_id_type=MESH,
-        )
-    lax.fori_loop(1, PEERS // 8, greet, 0)
+    columns = [column_ahead(c) for c in range(PEERS // 8)]
+    for c, dz in FAR_FIRST:
+        peer = columns[c] + z_ahead[dz]
+        pl.semaphore_signal(barrier, inc=1, device_id=(peer, feat), device_id_type=MESH)
     for load in loads[3:]:
         load.start()
     for load in loads[1:3]:
@@ -203,13 +197,13 @@
     for pair in pairs:
         pair.start()
 
-    def send_back(c, first):
+    def send_back(c, first, into=None, base_slot=0):
         base = column_behind(c)
         for dz in range(first, 8):
             peer = base + z_behind[dz]
             pltpu.make_async_remote_copy(
                 src_ref=stale_ref.at[peer],
-                dst_ref=back.at[c * 8 + dz],
+                dst_ref=(back if into is None else into).at[c * 8 + dz - base_slot],
                 send_sem=send_sem.at[1],
                 recv_sem=back_sem.at[c // 2],
                 device_id=(peer, feat),
@@ -221,7 +215,9 @@
         return carry
 
     send_back(0, 1)
-    lax.fori_loop(1, PEERS // 8, send_back_column, 0)
+    lax.fori_loop(1, PEERS // 8 - 2, send_back_column, 0)
+    for c in (PEERS // 8 - 2, PEERS // 8 - 1):
+        send_back(c, 0, last_ref, PEERS - GROUP)
 
     sub = lax.broadcasted_iota(jnp.int32, (BLOCK, BLOCK), 0)
     lanes = lax.broadcasted_iota(jnp.int32, (BLOCK, BLOCK), 1)
@@ -247,7 +243,7 @@
     meta_v[1:2, :] = jnp.where(col_here + 1 == col_before, 1, 0)
     meta_v[2:3, :] = jnp.maximum(count(down <= lanes) - 1, 0)
     meta_v[3:4, :] = jnp.minimum(count(down == lanes), 1)
-    meta_copy = pltpu.make_async_copy(meta_v, meta_s, out_sem.at[3])
+    meta_copy = pltpu.make_async_copy(meta_v, meta_s, out_sem.at[4])
     meta_copy.start()
     meta_copy.wait()
 
@@ -363,11 +359,7 @@
     bnd_copy = pltpu.make_async_copy(out_buf, bnd_ref, out_sem.at[1])
     bnd_copy.start()
 
-    def out_piece(p):
-        rows = pl.ds(pl.multiple_of(p * PIECE, PIECE), PIECE)
-        return pltpu.make_async_copy(prev.at[rows], grad_ref.at[rows], out_sem.at[2])
-
-    def scatter(g, first, last):
+    def mark_group(g):
         row = rows_of[g][0:1, :]
 
         def mark(p, carry):
@@ -377,58 +369,55 @@
             return carry
 
         lax.fori_loop(0, nodes // PIECE, mark, 0)
+
+    def scatter(g, first):
+        mark_group(g)
         arrived = back.at[pl.ds(0, GROUP - first)]
         pltpu.make_async_copy(arrived, arrived, back_sem.at[g]).wait()
         values = back[pl.ds(g * GROUP, GROUP)].astype(F32).reshape(SLOTS, -1).astype(BF16)
 
         def add(p, carry):
             rows = pl.ds(pl.multiple_of(p * PIECE, PIECE), PIECE)
-            added = total[rows, :] + jnp.dot(spread[rows, :], values, preferred_element_type=F32)
-            if last:
-                prev[rows, :] = added.astype(BF16)
-                out_piece(p).start()
-            else:
-                total[rows, :] = added
+            total[rows, :] += jnp.dot(spread[rows, :], values, preferred_element_type=F32)
             return carry
 
         lax.fori_loop(0, nodes // PIECE, add, 0)
 
-    scatter(0, 1, False)
+    scatter(0, 1)
 
     def scatter_group(g, carry):
-        scatter(g, 0, False)
+        scatter(g, 0)
         return carry
 
     lax.fori_loop(1, GROUPS - 1, scatter_group, 0)
-    scatter(GROUPS - 1, 0, True)
-    pltpu.make_async_copy(back.at[all_but_one], back.at[all_but_one], send_sem.at[1]).wait()
-    hid_copy.wait()
-    bnd_copy.wait()
-    pltpu.make_async_copy(prev, grad_ref, out_sem.at[2]).wait()
-
-
-def hand_over(
-    hid_in, grad_in, bnd_in, hid_out, grad_out, bnd_out, hid, grad, bnd, load_sem, store_sem
-):
-    loads, stores = [], []
-    triples = ((hid_in, hid, hid_out), (grad_in, grad, grad_out), (bnd_in, bnd, bnd_out))
-    for n, (src, held, dst) in enumerate(triples):
-        step = held.shape[0] // PARTS
-        for part in range(PARTS):
-            piece = pl.ds(part * step, step)
-            loads.append(
-                pltpu.make_async_copy(src.at[piece], held.at[piece], load_sem.at[n, part])
-            )
-            stores.append(
-                pltpu.make_async_copy(held.at[piece], dst.at[piece], store_sem.at[n, part])
-            )
-    for load in loads:
-        load.start()
-    for load, store in zip(loads, stores):
-        load.wait()
-        store.start()
-    for store in stores:
-        store.wait()
+
+    total_copy = pltpu.make_async_copy(total, total_ref, out_sem.at[2])
+    total_copy.start()
+    mark_group(GROUPS - 1)
+    spread_copy = pltpu.make_async_copy(spread, spread_ref, out_sem.at[3])
+    spread_copy.start()
+    pltpu.make_async_copy(last_ref, last_ref, back_sem.at[GROUPS - 1]).wait()
+    pltpu.make_async_copy(recv.at[all_but_one], recv.at[all_but_one], send_sem.at[1]).wait()
+    for copy in (hid_copy, bnd_copy, total_copy, spread_copy):
+        copy.wait()
+
+
+def finish_kernel(hid, bnd, total, spread, last, hid_out, grad_out, bnd_out, grad, sem):
+    whole = [
+        pltpu.make_async_copy(hid, hid_out, sem.at[0]),
+        pltpu.make_async_copy(bnd, bnd_out, sem.at[1]),
+    ]
+    for copy in whole:
+        copy.start()
+    values = last[...].astype(F32).reshape(SLOTS, -1).astype(BF16)
+    for p in range(grad.shape[0] // PIECE):
+        rows = pl.ds(p * PIECE, PIECE)
+        added = total[rows, :] + jnp.dot(spread[rows, :], values, preferred_element_type=F32)
+        grad[rows, :] = added.astype(BF16)
+        pltpu.make_async_copy(grad.at[rows], grad_out.at[rows], sem.at[2]).start()
+    for copy in whole:
+        copy.wait()
+    pltpu.make_async_copy(grad, grad_out, sem.at[2]).wait()
 
 
 def per_device(
@@ -450,13 +439,20 @@
     rows = jax.ShapeDtypeStruct((nodes, width), BF16)
     slots = jax.ShapeDtypeStruct((PEERS, CAP, width), BF16)
     anywhere = pl.BlockSpec(memory_space=pl.ANY)
+    vmem = pl.BlockSpec(memory_space=pltpu.VMEM)
     dma = pltpu.SemaphoreType.DMA
     whole = pltpu.VMEM((nodes, width), BF16)
     results = pl.pallas_call(
         layer_kernel,
-        out_shape=[rows, rows, slots],
+        out_shape=[
+            whole,
+            pltpu.VMEM((PEERS, CAP, width), BF16),
+            pltpu.VMEM((nodes, width), F32),
+            pltpu.VMEM((nodes, SLOTS), BF16),
+            pltpu.VMEM((GROUP, CAP, width), BF16),
+        ],
         in_specs=[anywhere] * 12,
-        out_specs=[anywhere] * 3,
+        out_specs=[anywhere] * 5,
         scratch_shapes=[
             pltpu.SMEM(tile_cols.shape, jnp.int32),
             pltpu.VMEM((CAP, PEERS), jnp.int32),
@@ -473,7 +469,7 @@
             pltpu.VMEM(adjacency.shape, BF16),
             pltpu.VMEM((PEERS, CAP, width), BF16),
             pltpu.VMEM((PEERS, CAP, width), BF16),
-            pltpu.VMEM((PEERS, CAP, width), BF16),
+            pltpu.VMEM((PEERS - GROUP, CAP, width), BF16),
             whole,
             whole,
             whole,
@@ -490,10 +486,10 @@
             dma((GROUPS,)),
             dma((CHUNKS + 5,)),
             dma((CHUNKS + 5,)),
-            dma((4,)),
+            dma((5,)),
         ],
         compiler_params=pltpu.CompilerParams(
-            collective_id=0, has_side_effects=True, vmem_limit_bytes=62 << 20
+            collective_id=0, has_side_effects=True, vmem_limit_bytes=53 << 20
         ),
     )(
         tile_cols,
@@ -510,19 +506,13 @@
         w_neigh,
     )
     return pl.pallas_call(
-        hand_over,
+        finish_kernel,
         out_shape=[rows, rows, slots],
-        in_specs=[anywhere] * 3,
+        in_specs=[vmem] * 5,
         out_specs=[anywhere] * 3,
-        scratch_shapes=[
-            whole,
-            whole,
-            pltpu.VMEM((PEERS, CAP, width), BF16),
-            dma((3, PARTS)),
-            dma((3, PARTS)),
-        ],
-        compiler_params=pltpu.CompilerParams(vmem_limit_bytes=62 << 20),
-    )(*results)
+        scratch_shapes=[whole, dma((3,))],
+        compiler_params=pltpu.CompilerParams(vmem_limit_bytes=FINISH_MB << 20),
+    )(*[pltpu.with_memory_space_constraint(result, pltpu.VMEM) for result in results])
 
 
 def solution(mesh):

time: 90.1 us -> 85.6 us (0.950)
  Pallas kernels: 89.3 us -> 84.8 us
    pallas_call x2, Pallas kernels: 89.3 us -> 84.8 us  [the longest x1 83 us: per_device(): pl.pallas_call(layer_kernel, out_shape=[whole, pltpu.VMEM((PEERS, CAP, wi...]
where the time goes in v4:
time: 85.6 us; the launch traced here: 85.5 us
  Pallas kernels  84.8 us (99%)
    pallas_call x1, Pallas kernels, per_device(): pl.pallas_call(layer_kernel, out_shape=[whole, pltpu.VMEM((PEERS, CAP, wi...  83 us
    pallas_call x1, Pallas kernels, per_device(): pl.pallas_call(finish_kernel, out_shape=[rows, rows, slots], in_specs=[vm...  1.86 us

profile of v4, /device:TPU:1, one launch (start us, length us, event | category | flops | bytes accessed | tf_op | source)
XLA Modules:
  0.0 85.5 jit_solution(11467209056250155762)
XLA Ops:
  0.6 83.0 %shard_map.139 = (bf16[2048,256]{1,0:T(8,128)(2,1)S(1)}, bf16[128,24,256]{2,1,0:T(8,128)(2,1)S(1)}, f32[2048,256]{1,0:T(8,128)S(1)}, bf16[2048,384]{1,0:T(8,128)(2,1)S(1)}, bf16[16,24,256]{2,1,0:T(8,128)(2,1)S(1)}) custom-call(s32[96]{0:T(128)} %tile_hbm.1, s32[24,128]{1,0:T(8,128)} %bitcast.6, s32[1,128]{1,0:T(1,128)} %bitcast.8, s32[1,128]{1,0:T(1,128)} %bitcast.9, ...), custom_call_target="tpu_custom_call" | custom-call | tf_op jit(solution)/shard_map/pallas_call | solution.py:445
  83.6 1.9 %shard_map.140 = (bf16[2048,256]{1,0:T(8,128)(2,1)}, bf16[2048,256]{1,0:T(8,128)(2,1)}, bf16[128,24,256]{2,1,0:T(8,128)(2,1)}) custom-call(bf16[2048,256]{1,0:T(8,128)(2,1)S(1)} %get-tuple-element.8.hid, bf16[128,24,256]{2,1,0:T(8,128)(2,1)S(1)} %get-tuple-element.9.bnd, f32[2048,256]{1,0:T(8,128)S(1)} %get-tuple-element.10.total, ...), custom_call_target="tpu_custom_call" | custom-call | tf_op jit(solution)/shard_map/pallas_call | solution.py:508

commit v5 on v4

--- a/solution.py
+++ b/solution.py
@@ -22,6 +22,7 @@
 FAR_FIRST = sorted(
     ((c, dz) for c in range(16) for dz in range(8) if c or dz), key=lambda at: -HOPS[at[0]][at[1]]
 )
+FAR_Z = (0, 4, 3, 5, 2, 6, 1, 7)
 CONTRACT_LAST = (((1,), (1,)), ((), ()))
 CONTRACT_FIRST = (((0,), (0,)), ((), ()))
 
@@ -114,7 +115,7 @@
                 (cot_ref, cot.at[feat]),
                 (ws_ref, ws.at[0]),
                 (wn_ref, wn.at[0]),
-                (stale_ref.at[me], back.at[0]),
+                (stale_ref.at[me], last_ref.at[0]),
             )
         )
     ]
@@ -167,7 +168,7 @@
             base = column_ahead(2 * g + half)
             if half == 0:
                 pl.when(g > 0)(lambda: send(base, g * GROUP, 0))
-            for dz in range(1 - half, 8):
+            for dz in FAR_Z[1 - half :]:
                 send(base, g * GROUP + half * 8 + dz, dz)
         return carry
 
@@ -197,13 +198,13 @@
     for pair in pairs:
         pair.start()
 
-    def send_back(c, first, into=None, base_slot=0):
+    def send_back(c, first, into, base_slot):
         base = column_behind(c)
-        for dz in range(first, 8):
+        for dz in FAR_Z[first:]:
             peer = base + z_behind[dz]
             pltpu.make_async_remote_copy(
                 src_ref=stale_ref.at[peer],
-                dst_ref=(back if into is None else into).at[c * 8 + dz - base_slot],
+                dst_ref=into.at[c * 8 + dz - base_slot],
                 send_sem=send_sem.at[1],
                 recv_sem=back_sem.at[c // 2],
                 device_id=(peer, feat),
@@ -211,13 +212,12 @@
             ).start()
 
     def send_back_column(c, carry):
-        send_back(c, 0)
-        return carry
-
-    send_back(0, 1)
-    lax.fori_loop(1, PEERS // 8 - 2, send_back_column, 0)
-    for c in (PEERS // 8 - 2, PEERS // 8 - 1):
-        send_back(c, 0, last_ref, PEERS - GROUP)
+        send_back(PEERS // 8 - 1 - c, 0, back, GROUP)
+        return carry
+
+    lax.fori_loop(0, PEERS // 8 - 2, send_back_column, 0)
+    send_back(1, 0, last_ref, 0)
+    send_back(0, 1, last_ref, 0)
 
     sub = lax.broadcasted_iota(jnp.int32, (BLOCK, BLOCK), 0)
     lanes = lax.broadcasted_iota(jnp.int32, (BLOCK, BLOCK), 1)
@@ -370,11 +370,12 @@
 
         lax.fori_loop(0, nodes // PIECE, mark, 0)
 
-    def scatter(g, first):
+    def scatter(n, carry):
+        g = GROUPS - 1 - n
         mark_group(g)
-        arrived = back.at[pl.ds(0, GROUP - first)]
+        arrived = back.at[pl.ds(0, GROUP)]
         pltpu.make_async_copy(arrived, arrived, back_sem.at[g]).wait()
-        values = back[pl.ds(g * GROUP, GROUP)].astype(F32).reshape(SLOTS, -1).astype(BF16)
+        values = back[pl.ds((g - 1) * GROUP, GROUP)].astype(F32).reshape(SLOTS, -1).astype(BF16)
 
         def add(p, carry):
             rows = pl.ds(pl.multiple_of(p * PIECE, PIECE), PIECE)
@@ -382,21 +383,17 @@
             return carry
 
         lax.fori_loop(0, nodes // PIECE, add, 0)
-
-    scatter(0, 1)
-
-    def scatter_group(g, carry):
-        scatter(g, 0)
-        return carry
-
-    lax.fori_loop(1, GROUPS - 1, scatter_group, 0)
+        return carry
+
+    lax.fori_loop(0, GROUPS - 1, scatter, 0)
 
     total_copy = pltpu.make_async_copy(total, total_ref, out_sem.at[2])
     total_copy.start()
-    mark_group(GROUPS - 1)
+    mark_group(0)
     spread_copy = pltpu.make_async_copy(spread, spread_ref, out_sem.at[3])
     spread_copy.start()
-    pltpu.make_async_copy(last_ref, last_ref, back_sem.at[GROUPS - 1]).wait()
+    arrived = last_ref.at[pl.ds(1, GROUP - 1)]
+    pltpu.make_async_copy(arrived, arrived, back_sem.at[0]).wait()
     pltpu.make_async_copy(recv.at[all_but_one], recv.at[all_but_one], send_sem.at[1]).wait()
     for copy in (hid_copy, bnd_copy, total_copy, spread_copy):
         copy.wait()

time: 85.6 us -> 84.6 us (0.988)
  Pallas kernels: 84.8 us -> 83.8 us
    pallas_call x1, Pallas kernels: 83 us -> 82 us  [per_device(): pl.pallas_call(layer_kernel, out_shape=[whole, pltpu.VMEM((PEERS, CAP, wi...]
where the time goes in v5:
time: 84.6 us; the launch traced here: 84.5 us
  Pallas kernels  83.8 us (99%)
    pallas_call x1, Pallas kernels, per_device(): pl.pallas_call(layer_kernel, out_shape=[whole, pltpu.VMEM((PEERS, CAP, wi...  82 us
    pallas_call x1, Pallas kernels, per_device(): pl.pallas_call(finish_kernel, out_shape=[rows, rows, slots], in_specs=[vm...  1.86 us

profile of v5, /device:TPU:1, one launch (start us, length us, event | category | flops | bytes accessed | tf_op | source)
XLA Modules:
  0.0 84.5 jit_solution(8945780280722324545)
XLA Ops:
  0.6 82.0 %shard_map.139 = (bf16[2048,256]{1,0:T(8,128)(2,1)S(1)}, bf16[128,24,256]{2,1,0:T(8,128)(2,1)S(1)}, f32[2048,256]{1,0:T(8,128)S(1)}, bf16[2048,384]{1,0:T(8,128)(2,1)S(1)}, bf16[16,24,256]{2,1,0:T(8,128)(2,1)S(1)}) custom-call(s32[96]{0:T(128)} %tile_hbm.1, s32[24,128]{1,0:T(8,128)} %bitcast.6, s32[1,128]{1,0:T(1,128)} %bitcast.8, s32[1,128]{1,0:T(1,128)} %bitcast.9, ...), custom_call_target="tpu_custom_call" | custom-call | tf_op jit(solution)/shard_map/pallas_call | solution.py:442
  82.6 1.9 %shard_map.140 = (bf16[2048,256]{1,0:T(8,128)(2,1)}, bf16[2048,256]{1,0:T(8,128)(2,1)}, bf16[128,24,256]{2,1,0:T(8,128)(2,1)}) custom-call(bf16[2048,256]{1,0:T(8,128)(2,1)S(1)} %get-tuple-element.8.hid, bf16[128,24,256]{2,1,0:T(8,128)(2,1)S(1)} %get-tuple-element.9.bnd, f32[2048,256]{1,0:T(8,128)S(1)} %get-tuple-element.10.total, ...), custom_call_target="tpu_custom_call" | custom-call | tf_op jit(solution)/shard_map/pallas_call | solution.py:505

commit v6 on v5

--- a/solution.py
+++ b/solution.py
@@ -18,7 +18,8 @@
 CHUNKS = 4
 FINISH_MB = 6
 PIECE = 256
-HOPS = [[min(c // 4, 4 - c // 4) + min(c % 4, 4 - c % 4) + min(z, 8 - z) for z in range(8)] for c in range(16)]
+NEAR = (0, 1, 2, 1)
+HOPS = [[NEAR[(c // 4 + 2 * (c % 4)) % 4] + NEAR[c % 4] + min(z, 8 - z) for z in range(8)] for c in range(16)]
 FAR_FIRST = sorted(
     ((c, dz) for c in range(16) for dz in range(8) if c or dz), key=lambda at: -HOPS[at[0]][at[1]]
 )
@@ -31,7 +32,8 @@
     z, x, y = lax.rem(me, 8), lax.rem(me // 8, 4), me // 32
 
     def column(c):
-        dy, dx = c // 4, lax.rem(c, 4)
+        dx = lax.rem(c, 4)
+        dy = lax.rem(c // 4 + 2 * dx, 4)
         if sign < 0:
             dy, dx = 4 - dy, 4 - dx
         return (lax.rem(y + dy, 4) * 4 + lax.rem(x + dx, 4)) * 8
@@ -141,7 +143,8 @@
 
     def gather(g, carry):
         i = g * GROUP + place
-        dz, dx, dy = i & 7, (i >> 3) & 3, i >> 5
+        dz, dx = i & 7, (i >> 3) & 3
+        dy = ((i >> 5) + 2 * dx) & 3
         z, x, y = me & 7, (me >> 3) & 3, me >> 5
         dest = (((y + dy) & 3) * 4 + ((x + dx) & 3)) * 8 + ((z + dz) & 7)
         column = jnp.sum(jnp.where(lane == dest, tiled, 0.0), axis=1, keepdims=True)

time: 84.6 us -> 84.7 us (level)
  no operation moved by 1% of the time
where the time goes in v6:
time: 84.7 us; the launch traced here: 84.6 us
  Pallas kernels  83.9 us (99%)
    pallas_call x1, Pallas kernels, per_device(): pl.pallas_call(layer_kernel, out_shape=[whole, pltpu.VMEM((PEERS, CAP, wi...  82.1 us
    pallas_call x1, Pallas kernels, per_device(): pl.pallas_call(finish_kernel, out_shape=[rows, rows, slots], in_specs=[vm...  1.86 us

profile of v6, /device:TPU:1, one launch (start us, length us, event | category | flops | bytes accessed | tf_op | source)
XLA Modules:
  0.0 84.6 jit_solution(3411617178401924278)
XLA Ops:
  0.6 82.1 %shard_map.139 = (bf16[2048,256]{1,0:T(8,128)(2,1)S(1)}, bf16[128,24,256]{2,1,0:T(8,128)(2,1)S(1)}, f32[2048,256]{1,0:T(8,128)S(1)}, bf16[2048,384]{1,0:T(8,128)(2,1)S(1)}, bf16[16,24,256]{2,1,0:T(8,128)(2,1)S(1)}) custom-call(s32[96]{0:T(128)} %tile_hbm.1, s32[24,128]{1,0:T(8,128)} %bitcast.6, s32[1,128]{1,0:T(1,128)} %bitcast.8, s32[1,128]{1,0:T(1,128)} %bitcast.9, ...), custom_call_target="tpu_custom_call" | custom-call | tf_op jit(solution)/shard_map/pallas_call | solution.py:445
  82.7 1.9 %shard_map.140 = (bf16[2048,256]{1,0:T(8,128)(2,1)}, bf16[2048,256]{1,0:T(8,128)(2,1)}, bf16[128,24,256]{2,1,0:T(8,128)(2,1)}) custom-call(bf16[2048,256]{1,0:T(8,128)(2,1)S(1)} %get-tuple-element.8.hid, bf16[128,24,256]{2,1,0:T(8,128)(2,1)S(1)} %get-tuple-element.9.bnd, f32[2048,256]{1,0:T(8,128)S(1)} %get-tuple-element.10.total, ...), custom_call_target="tpu_custom_call" | custom-call | tf_op jit(solution)/shard_map/pallas_call | solution.py:508
